TPU v7x, 32 devices: a whole 2x2x4 slice. The times are simulated.
32 devices in a mesh: groups: 2 (over y), ctx: 4 (over z), tp: 4 (over x, core).
Axes of the slice: x: 2, y: 2, z: 4, core: 2. Of those that a mesh axis runs over, the one named last changes fastest.
Arguments:
- inner_gate_proj: bfloat16 [4096, 2048], P('tp', ('groups', 'ctx')), parts along dimension 1, may hold values from -6 to 6
- outer_gate_proj: bfloat16 [4096, 2048], P('tp', ('groups', 'ctx')), parts along dimension 1, may hold values from -6 to 6
- value_projection: bfloat16 [4096, 2048], P('tp', ('groups', 'ctx')), parts along dimension 1, may hold values from -6 to 6
- channel_filter_lags: float32 [4096, 1024], P('tp', 'ctx'), may hold values from -0.1875 to 0.1875
- channel_filter_length: int32 [4096], P('tp'), may hold values from 128 to 1024, as said below
- output_cotangent: bfloat16 [2048, 8192], P(('groups', 'ctx'), 'tp'), parts along dimension 0, may hold values from -6 to 6
- output_weight: bfloat16 [4096, 8192], P('ctx', 'tp'), may hold values from -0.0625 to 0.0625
- adapter_down_factor: bfloat16 [4096, 32], P('tp'), may hold values from -1 to 1
- adapter_up_factor: bfloat16 [32, 8192], P(None, 'tp'), may hold values from -0.0625 to 0.0625
Outputs:
- inner_gate_gradient: bfloat16 [4096, 2048], P('tp', ('groups', 'ctx')), parts along dimension 1
- outer_gate_gradient: bfloat16 [4096, 2048], P('tp', ('groups', 'ctx')), parts along dimension 1
- value_gradient: bfloat16 [4096, 2048], P('tp', ('groups', 'ctx')), parts along dimension 1
- down_factor_gradient: float32 [8192, 32], P(('groups', 'tp')), parts along dimension 0
- up_factor_gradient: float32 [64, 8192], P('groups', 'tp'), parts along dimension 0
There are 2 independent parts, one for each index of `groups`. A program takes and returns all parts, laid end to end along the dimension named above; an argument that names none is the same for every part. Nothing has to cross between parts.
Inputs may be any that keep to these rules, and one draw needn't show every extreme that they name: `channel_filter_length`: equal to 1024 for some channel and to 128 for another.
All inputs are finite; a program needn't handle non-finite values.
Results may differ from a plain program's by a relative error of at most 0.017.
Values may be sent and summed in bfloat16 or wider, within the bound.
A program may use at most 128 MiB of HBM per device.

v0:
```python
import math

import jax
import jax.numpy as jnp
from jax import lax
from jax.sharding import PartitionSpec as P

adapter_scale = 2.0


def product_bf(left, right):
    return (left.astype(jnp.float32) * right.astype(jnp.float32)).astype(jnp.bfloat16)


def dft_table(length):
    across = lax.broadcasted_iota(jnp.int32, (length, length), 0)
    downward = lax.broadcasted_iota(jnp.int32, (length, length), 1)
    angle = -2.0 * math.pi / length * (across * downward % length).astype(jnp.float32)
    return (jnp.cos(angle), jnp.sin(angle))


def twiddle_table(outer, inner):
    total = outer * inner
    first_idx = lax.broadcasted_iota(jnp.int32, (outer, inner), 0)
    second_idx = lax.broadcasted_iota(jnp.int32, (outer, inner), 1)
    angle = -2.0 * math.pi / total * (first_idx * second_idx % total).astype(jnp.float32)
    return (jnp.cos(angle), jnp.sin(angle))


def left_apply(table, field):
    return jnp.einsum("ap,cpq->caq", table, field, precision=lax.Precision.HIGHEST)


def right_apply(field, table):
    return jnp.einsum("caq,qb->cab", field, table, precision=lax.Precision.HIGHEST)


def forward_dft(signal, tables):
    outer_cos, outer_sin, inner_cos, inner_sin, twist_cos, twist_sin = tables
    channels = signal.shape[0]
    block = signal.reshape(channels, outer_cos.shape[0], inner_cos.shape[0])
    first_real = left_apply(outer_cos, block)
    first_imag = left_apply(outer_sin, block)
    turned_real = first_real * twist_cos - first_imag * twist_sin
    turned_imag = first_real * twist_sin + first_imag * twist_cos
    spec_real = right_apply(turned_real, inner_cos) - right_apply(turned_imag, inner_sin)
    spec_imag = right_apply(turned_real, inner_sin) + right_apply(turned_imag, inner_cos)
    return (spec_real, spec_imag)


def inverse_real(spec_real, spec_imag, tables):
    outer_cos, outer_sin, inner_cos, inner_sin, twist_cos, twist_sin = tables
    back_real = right_apply(spec_real, inner_cos) + right_apply(spec_imag, inner_sin)
    back_imag = right_apply(spec_imag, inner_cos) - right_apply(spec_real, inner_sin)
    untwist_real = back_real * twist_cos + back_imag * twist_sin
    untwist_imag = back_imag * twist_cos - back_real * twist_sin
    result = left_apply(outer_cos, untwist_real) + left_apply(outer_sin, untwist_imag)
    total = outer_cos.shape[0] * inner_cos.shape[0]
    return result.reshape(result.shape[0], total) / total


def convolve(taps, gated, grad_conv):
    channels, length = taps.shape
    total = 2 * length
    outer = 1 << (total.bit_length() - 1) // 2
    inner = total // outer
    outer_cos, outer_sin = dft_table(outer)
    inner_cos, inner_sin = dft_table(inner)
    twist_cos, twist_sin = twiddle_table(outer, inner)
    tables = (outer_cos, outer_sin, inner_cos, inner_sin, twist_cos, twist_sin)
    padding = jnp.zeros((channels, length), jnp.float32)

    def spectrum(field):
        return forward_dft(jnp.concatenate([field.astype(jnp.float32), padding], axis=1), tables)

    filt_real, filt_imag = spectrum(taps)
    gated_real, gated_imag = spectrum(gated)
    grad_real, grad_imag = spectrum(grad_conv)
    forward_val = inverse_real(
        filt_real * gated_real - filt_imag * gated_imag,
        filt_real * gated_imag + filt_imag * gated_real,
        tables,
    )[:, :length]
    backward_val = inverse_real(
        filt_real * grad_real + filt_imag * grad_imag,
        filt_real * grad_imag - filt_imag * grad_real,
        tables,
    )[:, :length]
    return (forward_val.astype(jnp.bfloat16), backward_val.astype(jnp.bfloat16))


def local(
    inner_gate_proj,
    outer_gate_proj,
    value_projection,
    channel_filter_lags,
    channel_filter_length,
    output_cotangent,
    output_weight,
    adapter_down_factor,
    adapter_up_factor,
):
    tok_rows = inner_gate_proj.shape[1]
    lag_index = lax.axis_index("ctx") * tok_rows + lax.broadcasted_iota(
        jnp.int32, channel_filter_lags.shape, 1
    )
    masked_filter = jnp.where(
        lag_index < channel_filter_length[:, None],
        channel_filter_lags,
        jnp.zeros_like(channel_filter_lags),
    )
    adapter_portion = lax.dot_general(
        output_cotangent,
        adapter_up_factor,
        (((1,), (1,)), ((), ())),
        preferred_element_type=jnp.float32,
    )
    adapter_backward = lax.psum(adapter_portion.astype(jnp.bfloat16), "tp").astype(jnp.float32)
    whole_weight = lax.all_gather(output_weight, "ctx", axis=0, tiled=True)
    output_backward = lax.psum_scatter(
        lax.dot_general(
            whole_weight,
            output_cotangent,
            (((1,), (1,)), ((), ())),
            preferred_element_type=jnp.float32,
        ).astype(jnp.bfloat16),
        "tp",
        scatter_dimension=0,
        tiled=True,
    ).astype(jnp.float32)
    adapter_term = lax.dot_general(
        adapter_down_factor.astype(jnp.float32),
        adapter_backward,
        (((1,), (1,)), ((), ())),
        precision=lax.Precision.HIGHEST,
    )
    projected_gradient = (output_backward + adapter_term).astype(jnp.bfloat16)
    gated = product_bf(inner_gate_proj, value_projection)
    grad_conv = product_bf(projected_gradient, outer_gate_proj)
    filter_channels = lax.all_to_all(
        masked_filter.astype(jnp.bfloat16), "ctx", split_axis=0, concat_axis=1, tiled=True
    ).astype(masked_filter.dtype)
    gated_ch, grad_conv_ch = (
        lax.all_to_all(gated, "ctx", split_axis=0, concat_axis=1, tiled=True),
        lax.all_to_all(grad_conv, "ctx", split_axis=0, concat_axis=1, tiled=True),
    )
    conv_ch, grad_gated_ch = convolve(filter_channels, gated_ch, grad_conv_ch)
    conv_out, grad_gated = (
        lax.all_to_all(conv_ch, "ctx", split_axis=1, concat_axis=0, tiled=True),
        lax.all_to_all(grad_gated_ch, "ctx", split_axis=1, concat_axis=0, tiled=True),
    )
    inner_gate_gradient = product_bf(grad_gated, value_projection)
    outer_gate_gradient = product_bf(projected_gradient, conv_out)
    value_gradient = product_bf(grad_gated, inner_gate_proj)
    block_output = product_bf(outer_gate_proj, conv_out)
    token_part = lax.dot_general(
        block_output,
        adapter_down_factor,
        (((0,), (0,)), ((), ())),
        preferred_element_type=jnp.float32,
    )
    token_adapter_rows = lax.psum(token_part.astype(jnp.bfloat16), "tp").astype(jnp.float32)
    down_portion = jnp.dot(
        block_output.astype(jnp.float32), adapter_backward, precision=lax.Precision.HIGHEST
    )
    part_b = lax.dot_general(
        token_adapter_rows,
        output_cotangent.astype(jnp.float32),
        (((0,), (0,)), ((), ())),
        precision=lax.Precision.HIGHEST,
    )
    down_factor_sum, up_factor_sum = (
        lax.psum(down_portion.astype(jnp.bfloat16), "ctx").astype(jnp.float32),
        lax.psum(part_b.astype(jnp.bfloat16), "ctx").astype(jnp.float32),
    )
    return (
        inner_gate_gradient,
        outer_gate_gradient,
        value_gradient,
        down_factor_sum * adapter_scale,
        up_factor_sum * adapter_scale,
    )


def solution(mesh):
    return jax.shard_map(
        local,
        mesh=mesh,
        in_specs=(
            P("tp", ("groups", "ctx")),
            P("tp", ("groups", "ctx")),
            P("tp", ("groups", "ctx")),
            P("tp", "ctx"),
            P("tp"),
            P(("groups", "ctx"), "tp"),
            P("ctx", "tp"),
            P("tp", None),
            P(None, "tp"),
        ),
        out_specs=(
            P("tp", ("groups", "ctx")),
            P("tp", ("groups", "ctx")),
            P("tp", ("groups", "ctx")),
            P(("groups", "tp"), None),
            P("groups", "tp"),
        ),
        check_vma=False,
    )
```

profile of v0, /device:TPU:0, one launch (start us, length us, event | category | flops | bytes accessed | tf_op | source)
XLA Modules:
  0.0 491.0 jit_solution(13336452397655025341)
XLA Ops:
  7.2 0.7 all-gather.2.cloned.1.call-update
  8.5 1.0 select_convert_fusion
  9.5 6.3 %all-to-all-start = ((bf16[4,256,256]{2,1,0:T(8,128)(2,1)}), bf16[4,256,256]{2,1,0:T(8,128)(2,1)S(1)}, u32[]{:S(2)}, u32[]{:S(2)}) async-start(bf16[4,256,256]{2,1,0:T(8,128)(2,1)} %bitcast), calls=%async_computation | async-start | bytes 1048576 | tf_op jit(solution)/shard_map/all_to_all | solution.py:140
  15.8 0.9 fusion.80
  16.8 27.5 %all-to-all-done = bf16[4,256,256]{2,1,0:T(8,128)(2,1)S(1)} async-done(((bf16[4,256,256]{2,1,0:T(8,128)(2,1)}), bf16[4,256,256]{2,1,0:T(8,128)(2,1)S(1)}, u32[]{:S(2)}, u32[]{:S(2)}) %all-to-all-start) | async-done | bytes 524320 | tf_op jit(solution)/shard_map/all_to_all | solution.py:140
  44.3 4.3 all-to-all-start.3
  48.7 1.0 copy.66
  49.7 28.6 %all-to-all-done.3 = bf16[4,256,256]{2,1,0:T(8,128)(2,1)S(1)} async-done(((bf16[4,256,256]{2,1,0:T(8,128)(2,1)}), bf16[4,256,256]{2,1,0:T(8,128)(2,1)S(1)}, u32[]{:S(2)}, u32[]{:S(2)}) %all-to-all-start.3) | async-done | bytes 524320 | tf_op jit(solution)/shard_map/all_to_all | solution.py:144
  78.5 1.1 concatenate.9
  79.7 1.3 fusion.98
  81.0 1.3 fusion.100
  82.4 1.3 fusion.92
  83.7 2.1 fusion
  85.8 3.3 fusion.22
  89.2 3.9 fusion.24
  93.0 4.7 fusion.38
  97.7 3.4 fusion.40
  101.1 4.7 fusion.58
  105.7 4.9 fusion.61
  110.6 3.3 fusion.46
  114.0 198.0 %all-gather.2.cloned.1.call-done = bf16[4096,2048]{1,0:T(8,128)(2,1)} async-done(((bf16[1024,2048]{1,0:T(8,128)(2,1)}), bf16[4096,2048]{1,0:T(8,128)(2,1)}) %all-gather.2.cloned.1.call-update) | async-done | bytes 16777232 | tf_op jit(solution)/shard_map/all_gather | solution.py:119
  312.0 9.9 %convolution_convert_fusion = bf16[4096,256]{1,0:T(8,128)(2,1)} fusion(bf16[4096,2048]{1,0:T(8,128)(2,1)} %all-gather.2.cloned.1.call-done, bf16[256,2048]{1,0:T(8,128)(2,1)S(1)} %copy-done), kind=kOutput, calls=%fused_computation | convolution fusion | flops 4296015872 | bytes 19922944 | tf_op jit(solution)/shard_map/dot_general | solution.py:121
  321.9 8.8 %multiply_subtract_fusion = (f32[256,32,64]{0,2,1:T(8,128)S(1)}, f32[256,32,64]{0,2,1:T(8,128)S(1)}, f32[256,32,64]{0,2,1:T(8,128)}) fusion(f32[256,32,64]{0,2,1:T(8,128)} %fusion.61, f32[256,32,64]{0,2,1:T(8,128)S(1)} %fusion.46, f32[256,32,64]{0,2,1:T(8,128)} %fusion.58, f32[256,32,64]{0,2,1:T(8,128)} %fusion.38, f32[256,32,64]{0,1,2:T(8,128)} %copy-done.1), kind=kOutput, calls=%fused_computation.34 | convolution fusion | flops 406380544 | bytes 16777216 | tf_op jit(solution)/shard_map/caq,qb->cab/dot_general | solution.py:35
  330.7 2.1 fusion.108
  332.8 2.1 fusion.124
  335.0 2.1 fusion.122
  337.2 2.6 fusion.110
  339.8 6.8 %fusion.6 = f32[256,64,32]{0,2,1:T(8,128)S(1)} fusion(f32[32,64]{0,1:T(8,128)S(1)} %get-tuple-element.26, f32[32,64]{0,1:T(8,128)S(1)} %get-tuple-element.27, f32[256,32,64]{0,2,1:T(8,128)S(1)} %fusion.110, f32[256,32,64]{0,2,1:T(8,128)S(1)} %fusion.124, f32[256,32,64]{0,2,1:T(8,128)S(1)} %fusion.108, f32[256,32,64]{0,2,1:T(8,128)S(1)} %fusion.122), kind=kOutput, calls=%fused_computation.25 | convolution fusion | flops 203962368 | bytes 10502144 | tf_op jit(solution)/shard_map/ap,cpq->caq/dot_general | solution.py:31
  346.6 9.0 %fusion.71 = bf16[256,32,64]{0,1,2:T(8,128)(2,1)S(1)} fusion(f32[256,64,32]{0,2,1:T(8,128)S(1)} %fusion.6, f32[32,64]{0,1:T(8,128)S(1)} %get-tuple-element.26, f32[32,64]{0,1:T(8,128)S(1)} %get-tuple-element.27, f32[256,32,64]{0,2,1:T(8,128)S(1)} %fusion.110, f32[256,32,64]{0,2,1:T(8,128)S(1)} %fusion.124, f32[256,32,64]{0,2,1:T(8,128)S(1)} %fusion.108, ...), kind=kOutput, calls=%fused_computation.77 | convolution fusion | flops 205535232 | bytes 11550720 | tf_op jit(solution)/shard_map/ap,cpq->caq/dot_general | solution.py:31
  355.6 0.6 copy.98
  356.2 0.8 slice.11
  357.0 4.1 all-to-all-start.4
  361.6 14.6 %all-to-all-done.4 = bf16[256,4,256]{0,2,1:T(8,128)(2,1)} async-done(((bf16[256,4,256]{0,2,1:T(8,128)(2,1)}), bf16[256,4,256]{0,2,1:T(8,128)(2,1)}, u32[]{:S(2)}, u32[]{:S(2)}) %all-to-all-start.4) | async-done | bytes 524320 | tf_op jit(solution)/shard_map/all_to_all | solution.py:149
  376.2 2.1 convert_bitcast_fusion
  378.3 2.6 copy.99
  380.9 1.5 fusion.78
  382.4 0.8 copy-done.3
  383.4 10.5 %all-reduce.3 = (bf16[256,32]{0,1:T(8,128)(2,1)S(1)}, bf16[256,32]{0,1:T(8,128)(2,1)S(1)}) all-reduce(bf16[256,32]{0,1:T(8,128)(2,1)S(1)} %convolution_convert_fusion.3, bf16[256,32]{0,1:T(8,128)(2,1)S(1)} %convolution_convert_fusion.4), channel_id=1, replica_groups=mesh['groups'=2,'ctx'=4,'tp'=4] {'tp'}, use_global_device_ids=true, to_apply=%region_1.2 | all-reduce | flops 16384 | bytes 65536 | tf_op jit(solution)/shard_map/psum | solution.py:118
  394.0 2.9 fusion.76
  396.9 2.0 copy.72
  398.9 4.1 all-to-all-start.1
  403.3 1.9 convolution_convert_fusion.2
  405.2 0.9 convolution_convert_fusion.1
  406.2 13.2 %all-to-all-done.1 = bf16[4,256,256]{1,2,0:T(8,128)(2,1)} async-done(((bf16[4,256,256]{1,2,0:T(8,128)(2,1)}), bf16[4,256,256]{1,2,0:T(8,128)(2,1)}, u32[]{:S(2)}, u32[]{:S(2)}) %all-to-all-start.1) | async-done | bytes 524320 | tf_op jit(solution)/shard_map/all_to_all | solution.py:145
  419.4 1.1 concatenate.10
  420.5 1.3 fusion.96
  421.9 2.1 fusion.2
  424.0 3.3 fusion.30
  427.3 3.3 fusion.32
  430.6 3.5 fusion.52
  434.2 3.9 multiply_add_fusion.1
  438.1 2.1 fusion.114
  440.3 2.1 fusion.130
  442.4 2.1 fusion.128
  444.6 2.5 fusion.116
  447.1 6.8 %fusion.14 = f32[256,64,32]{0,2,1:T(8,128)S(1)} fusion(f32[32,64]{0,1:T(8,128)S(1)} %get-tuple-element.26, f32[32,64]{0,1:T(8,128)S(1)} %get-tuple-element.27, f32[256,32,64]{0,2,1:T(8,128)S(1)} %fusion.116, f32[256,32,64]{0,2,1:T(8,128)S(1)} %fusion.130, f32[256,32,64]{0,2,1:T(8,128)S(1)} %fusion.114, f32[256,32,64]{0,2,1:T(8,128)S(1)} %fusion.128), kind=kOutput, calls=%fused_computation.36 | convolution fusion | flops 203962368 | bytes 10502144 | tf_op jit(solution)/shard_map/ap,cpq->caq/dot_general | solution.py:31
  454.0 9.2 %fusion.68 = bf16[256,32,64]{0,1,2:T(8,128)(2,1)S(1)} fusion(f32[256,64,32]{0,2,1:T(8,128)S(1)} %fusion.14, f32[32,64]{0,1:T(8,128)S(1)} %get-tuple-element.26, f32[32,64]{0,1:T(8,128)S(1)} %get-tuple-element.27, f32[256,32,64]{0,2,1:T(8,128)S(1)} %fusion.116, f32[256,32,64]{0,2,1:T(8,128)S(1)} %fusion.130, f32[256,32,64]{0,2,1:T(8,128)S(1)} %fusion.114, ...), kind=kOutput, calls=%fused_computation.76 | convolution fusion | flops 205535232 | bytes 11550720 | tf_op jit(solution)/shard_map/ap,cpq->caq/dot_general | solution.py:31
  463.1 0.6 copy.85
  463.7 0.8 slice.10
  464.6 3.5 all-to-all-start.2
  468.1 1.5 convert_multiply_fusion.7
  469.6 1.6 convert_multiply_fusion.6
  471.2 10.2 %all-to-all-done.2 = bf16[256,4,256]{0,2,1:T(8,128)(2,1)S(1)} async-done(((bf16[256,4,256]{0,2,1:T(8,128)(2,1)}), bf16[256,4,256]{0,2,1:T(8,128)(2,1)S(1)}, u32[]{:S(2)}, u32[]{:S(2)}) %all-to-all-start.2) | async-done | bytes 524320 | tf_op jit(solution)/shard_map/all_to_all | solution.py:150
  481.8 2.4 fusion.81
  (34 shorter events, 2.3 us)
Async XLA Ops:
  7.2 304.8 %copy-start = (bf16[256,2048]{1,0:T(8,128)(2,1)S(1)}, bf16[256,2048]{1,0:T(8,128)(2,1)}, u32[]{:S(2)}) copy-start(bf16[256,2048]{1,0:T(8,128)(2,1)} %param.14) | copy-start | bytes 3145732
  7.2 0.8 copy-start.9
  7.2 1.3 copy-start.6
  7.2 304.8 %all-gather.2.cloned.1.call-start = ((), (), s32[]{:S(2)}) async-start(), calls=%async_computation.6 | async-start | bytes 20971520 | tf_op jit(solution)/shard_map/all_gather | solution.py:119
  7.9 7.9 %copy-start.4 = (bf16[1024,256]{1,0:T(8,128)(2,1)S(1)}, bf16[1024,256]{1,0:T(8,128)(2,1)}, u32[]{:S(2)}) copy-start(bf16[1024,256]{1,0:T(8,128)(2,1)} %param.9) | copy-start | bytes 1572868
  7.9 7.9 %copy-start.5 = (bf16[1024,256]{1,0:T(8,128)(2,1)S(1)}, bf16[1024,256]{1,0:T(8,128)(2,1)}, u32[]{:S(2)}) copy-start(bf16[1024,256]{1,0:T(8,128)(2,1)} %param.11) | copy-start | bytes 1572868
  9.5 34.7 %all-to-all-start = ((bf16[4,256,256]{2,1,0:T(8,128)(2,1)}), bf16[4,256,256]{2,1,0:T(8,128)(2,1)S(1)}, u32[]{:S(2)}, u32[]{:S(2)}) async-start(bf16[4,256,256]{2,1,0:T(8,128)(2,1)} %bitcast), calls=%async_computation | async-start | bytes 1048576 | tf_op jit(solution)/shard_map/all_to_all | solution.py:140
  44.3 34.0 %all-to-all-start.3 = ((bf16[4,256,256]{2,1,0:T(8,128)(2,1)}), bf16[4,256,256]{2,1,0:T(8,128)(2,1)S(1)}, u32[]{:S(2)}, u32[]{:S(2)}) async-start(bf16[4,256,256]{2,1,0:T(8,128)(2,1)} %bitcast.22), calls=%async_computation.4 | async-start | bytes 1048576 | tf_op jit(solution)/shard_map/all_to_all | solution.py:144
  48.5 345.5 %reduce-scatter.2.cloned.1.call-start = ((), (), s32[]{:S(2)}) async-start(), calls=%async_computation.7 | async-start | bytes 2621440 | tf_op jit(solution)/shard_map/reduce_scatter | solution.py:120
  85.8 24.8 %copy-start.1 = (f32[256,32,64]{0,1,2:T(8,128)}, f32[256,32,64]{0,1,2:T(8,128)S(1)}, u32[]{:S(2)}) copy-start(f32[256,32,64]{0,1,2:T(8,128)S(1)} %get-tuple-element.24) | copy-start | bytes 6291460
  355.6 5.6 %copy-start.8 = (bf16[32,2048]{1,0:T(8,128)(2,1)S(1)}, bf16[32,2048]{1,0:T(8,128)(2,1)}, u32[]{:S(2)}) copy-start(bf16[32,2048]{1,0:T(8,128)(2,1)} %param.17) | copy-start | bytes 393220
  357.0 19.2 %all-to-all-start.4 = ((bf16[256,4,256]{0,2,1:T(8,128)(2,1)}), bf16[256,4,256]{0,2,1:T(8,128)(2,1)}, u32[]{:S(2)}, u32[]{:S(2)}) async-start(bf16[256,4,256]{0,2,1:T(8,128)(2,1)} %bitcast.183), calls=%async_computation.5 | async-start | bytes 1048576 | tf_op jit(solution)/shard_map/all_to_all | solution.py:149
  378.3 4.9 copy-start.7
  382.4 0.8 copy-start.3
  398.9 20.5 %all-to-all-start.1 = ((bf16[4,256,256]{1,2,0:T(8,128)(2,1)}), bf16[4,256,256]{1,2,0:T(8,128)(2,1)}, u32[]{:S(2)}, u32[]{:S(2)}) async-start(bf16[4,256,256]{1,2,0:T(8,128)(2,1)} %copy.72), calls=%async_computation.2 | async-start | bytes 1048576 | tf_op jit(solution)/shard_map/all_to_all | solution.py:145
  403.1 65.0 %all-reduce.7.cloned.1.call-start = ((), (), s32[]{:S(2)}) async-start(), calls=%async_computation.8 | async-start | bytes 393216 | tf_op jit(solution)/shard_map/psum | solution.py:173
  430.6 3.6 copy-start.2
  464.6 16.8 %all-to-all-start.2 = ((bf16[256,4,256]{0,2,1:T(8,128)(2,1)}), bf16[256,4,256]{0,2,1:T(8,128)(2,1)S(1)}, u32[]{:S(2)}, u32[]{:S(2)}) async-start(bf16[256,4,256]{0,2,1:T(8,128)(2,1)} %bitcast.19), calls=%async_computation.3 | async-start | bytes 1048576 | tf_op jit(solution)/shard_map/all_to_all | solution.py:150
Sparse Core Ops, SparseCore 0:
  9.6 302.3 all-gather.1
  322.0 30.4 reduce-scatter.1
  407.0 36.8 all-reduce.6
where the time goes:
time: 501 us; the launch traced here: 491 us
  waiting for transfers between devices  293 us (58%)
  matrix products  127 us (25%)
  starting transfers between devices  22.6 us (5%)
  between operations  14.4 us (3%)
  local copies, waits for them, and re-layouts  12.7 us (3%)
  other arithmetic  11.3 us (2%)
  blocking collectives  10.5 us (2%)
    all_gather x1, waiting for transfers between devices, local(): whole_weight = lax.all_gather(output_weight, 'ctx', axis=0, tiled=True)  198 us
    dot_general x20, matrix products, right_apply(): jnp.einsum('caq,qb->cab', field, table, precision=lax.Precision.HIGHEST)  69 us
    dot_general x10, matrix products, left_apply(): jnp.einsum('ap,cpq->caq', table, field, precision=lax.Precision.HIGHEST)  41.4 us
    all_to_all x1, waiting for transfers between devices, local(): lax.all_to_all(gated, 'ctx', split_axis=0, concat_axis=1, tiled=True)  28.6 us
    all_to_all x1, waiting for transfers between devices, local(): lax.all_to_all(masked_filter.astype(jnp.bfloat16), 'ctx', split_axis=0, c...  27.5 us
    all_to_all x1, waiting for transfers between devices, local(): lax.all_to_all(conv_ch, 'ctx', split_axis=1, concat_axis=0, tiled=True)  14.6 us
    all_to_all x1, waiting for transfers between devices, local(): lax.all_to_all(grad_conv, 'ctx', split_axis=0, concat_axis=1, tiled=True)  13.2 us
    psum x1, blocking collectives, local(): lax.psum(adapter_portion.astype(jnp.bfloat16), 'tp').astype(jnp.float32)  10.5 us
  transfers between devices with their start and end apart: 8, of which 6 were waited for; matrix products, arithmetic and copies ran while one was open for 27% of the time, Pallas kernels for 0%

commit v1 on v0

--- a/solution.py
+++ b/solution.py
@@ -2,6 +2,8 @@
 
 import jax
 import jax.numpy as jnp
+import ml_dtypes
+import numpy as np
 from jax import lax
 from jax.sharding import PartitionSpec as P
 
@@ -89,6 +91,48 @@
     return (forward_val.astype(jnp.bfloat16), backward_val.astype(jnp.bfloat16))
 
 
+dense_length = 2048
+
+
+def dense_table(length):
+    lag = np.arange(length, dtype=np.int64)[:, None]
+    freq = np.arange(length, dtype=np.int64)[None, :]
+    angle = np.pi / (2 * length) * (lag * (2 * freq + 1) % (4 * length))
+    table = np.concatenate([np.cos(angle), np.sin(angle)], axis=1)
+    return jnp.asarray(table.astype(ml_dtypes.bfloat16))
+
+
+def dense_spectrum(field, table):
+    spec = jnp.dot(field, table, preferred_element_type=jnp.float32)
+    return spec[:, : field.shape[1]], spec[:, field.shape[1] :]
+
+
+def dense_inverse(cos_part, sin_part, table):
+    spec = jnp.concatenate([cos_part, sin_part], axis=1).astype(jnp.bfloat16)
+    field = lax.dot_general(
+        spec, table, (((1,), (1,)), ((), ())), preferred_element_type=jnp.float32
+    )
+    return (field * (1.0 / table.shape[0])).astype(jnp.bfloat16)
+
+
+def convolve_dense(taps, gated, grad_conv):
+    table = dense_table(taps.shape[1])
+    filt_cos, filt_sin = dense_spectrum(taps, table)
+    gated_cos, gated_sin = dense_spectrum(gated, table)
+    conv = dense_inverse(
+        filt_cos * gated_cos - filt_sin * gated_sin,
+        filt_cos * gated_sin + filt_sin * gated_cos,
+        table,
+    )
+    grad_cos, grad_sin = dense_spectrum(grad_conv, table)
+    back = dense_inverse(
+        filt_cos * grad_cos + filt_sin * grad_sin,
+        filt_cos * grad_sin - filt_sin * grad_cos,
+        table,
+    )
+    return conv, back
+
+
 def local(
     inner_gate_proj,
     outer_gate_proj,
@@ -100,6 +144,7 @@
     adapter_down_factor,
     adapter_up_factor,
 ):
+    ctx_size, tp_size = lax.axis_size("ctx"), lax.axis_size("tp")
     tok_rows = inner_gate_proj.shape[1]
     lag_index = lax.axis_index("ctx") * tok_rows + lax.broadcasted_iota(
         jnp.int32, channel_filter_lags.shape, 1
@@ -108,77 +153,80 @@
         lag_index < channel_filter_length[:, None],
         channel_filter_lags,
         jnp.zeros_like(channel_filter_lags),
-    )
-    adapter_portion = lax.dot_general(
-        output_cotangent,
-        adapter_up_factor,
+    ).astype(jnp.bfloat16)
+    gated = product_bf(inner_gate_proj, value_projection)
+    whole_cotangent = lax.all_gather(output_cotangent, "ctx", axis=0, tiled=True)
+    filter_ch, gated_ch, outer_ch = lax.all_to_all(
+        jnp.stack([masked_filter, gated, outer_gate_proj]),
+        "ctx",
+        split_axis=1,
+        concat_axis=2,
+        tiled=True,
+    )
+    rows = filter_ch.shape[0]
+    down_rows = lax.dynamic_slice_in_dim(
+        adapter_down_factor, lax.axis_index("ctx") * rows, rows, axis=0
+    )
+    partial = lax.dot_general(
+        output_weight,
+        whole_cotangent,
         (((1,), (1,)), ((), ())),
         preferred_element_type=jnp.float32,
-    )
-    adapter_backward = lax.psum(adapter_portion.astype(jnp.bfloat16), "tp").astype(jnp.float32)
-    whole_weight = lax.all_gather(output_weight, "ctx", axis=0, tiled=True)
-    output_backward = lax.psum_scatter(
+    ).astype(jnp.bfloat16)
+    adapter_backward = lax.psum(
         lax.dot_general(
-            whole_weight,
-            output_cotangent,
+            whole_cotangent,
+            adapter_up_factor,
             (((1,), (1,)), ((), ())),
             preferred_element_type=jnp.float32,
         ).astype(jnp.bfloat16),
         "tp",
-        scatter_dimension=0,
-        tiled=True,
-    ).astype(jnp.float32)
+    )
+    scattered = lax.psum_scatter(partial, "tp", scatter_dimension=0, tiled=True)
+    moves = [(i, (i % ctx_size) * tp_size + i // ctx_size) for i in range(ctx_size * tp_size)]
+    output_backward = lax.ppermute(scattered, ("ctx", "tp"), moves).astype(jnp.float32)
     adapter_term = lax.dot_general(
-        adapter_down_factor.astype(jnp.float32),
+        down_rows,
         adapter_backward,
         (((1,), (1,)), ((), ())),
-        precision=lax.Precision.HIGHEST,
+        preferred_element_type=jnp.float32,
     )
     projected_gradient = (output_backward + adapter_term).astype(jnp.bfloat16)
-    gated = product_bf(inner_gate_proj, value_projection)
-    grad_conv = product_bf(projected_gradient, outer_gate_proj)
-    filter_channels = lax.all_to_all(
-        masked_filter.astype(jnp.bfloat16), "ctx", split_axis=0, concat_axis=1, tiled=True
-    ).astype(masked_filter.dtype)
-    gated_ch, grad_conv_ch = (
-        lax.all_to_all(gated, "ctx", split_axis=0, concat_axis=1, tiled=True),
-        lax.all_to_all(grad_conv, "ctx", split_axis=0, concat_axis=1, tiled=True),
-    )
-    conv_ch, grad_gated_ch = convolve(filter_channels, gated_ch, grad_conv_ch)
-    conv_out, grad_gated = (
-        lax.all_to_all(conv_ch, "ctx", split_axis=1, concat_axis=0, tiled=True),
-        lax.all_to_all(grad_gated_ch, "ctx", split_axis=1, concat_axis=0, tiled=True),
-    )
-    inner_gate_gradient = product_bf(grad_gated, value_projection)
-    outer_gate_gradient = product_bf(projected_gradient, conv_out)
-    value_gradient = product_bf(grad_gated, inner_gate_proj)
-    block_output = product_bf(outer_gate_proj, conv_out)
+    grad_conv = product_bf(projected_gradient, outer_ch)
+    if filter_ch.shape[1] <= dense_length:
+        conv_ch, grad_gated_ch = convolve_dense(filter_ch, gated_ch, grad_conv)
+    else:
+        conv_ch, grad_gated_ch = convolve(filter_ch.astype(jnp.float32), gated_ch, grad_conv)
+    block_output = product_bf(outer_ch, conv_ch)
     token_part = lax.dot_general(
         block_output,
-        adapter_down_factor,
+        down_rows,
         (((0,), (0,)), ((), ())),
         preferred_element_type=jnp.float32,
     )
-    token_adapter_rows = lax.psum(token_part.astype(jnp.bfloat16), "tp").astype(jnp.float32)
-    down_portion = jnp.dot(
-        block_output.astype(jnp.float32), adapter_backward, precision=lax.Precision.HIGHEST
-    )
-    part_b = lax.dot_general(
-        token_adapter_rows,
-        output_cotangent.astype(jnp.float32),
+    token_adapter = lax.psum(token_part.astype(jnp.bfloat16), ("ctx", "tp"))
+    outer_grad_ch = product_bf(projected_gradient, conv_ch)
+    grad_gated, outer_gate_gradient = lax.all_to_all(
+        jnp.stack([grad_gated_ch, outer_grad_ch]),
+        "ctx",
+        split_axis=2,
+        concat_axis=1,
+        tiled=True,
+    )
+    down_part = jnp.dot(block_output, adapter_backward, preferred_element_type=jnp.float32)
+    down_sum = lax.all_gather(down_part.astype(jnp.bfloat16), "ctx", axis=0, tiled=True)
+    up_sum = lax.dot_general(
+        token_adapter,
+        whole_cotangent,
         (((0,), (0,)), ((), ())),
-        precision=lax.Precision.HIGHEST,
-    )
-    down_factor_sum, up_factor_sum = (
-        lax.psum(down_portion.astype(jnp.bfloat16), "ctx").astype(jnp.float32),
-        lax.psum(part_b.astype(jnp.bfloat16), "ctx").astype(jnp.float32),
+        preferred_element_type=jnp.float32,
     )
     return (
-        inner_gate_gradient,
+        product_bf(grad_gated, value_projection),
         outer_gate_gradient,
-        value_gradient,
-        down_factor_sum * adapter_scale,
-        up_factor_sum * adapter_scale,
+        product_bf(grad_gated, inner_gate_proj),
+        down_sum.astype(jnp.float32) * adapter_scale,
+        up_sum * adapter_scale,
     )
 
 

time: 501 us -> 345 us (0.69); the launches traced: 491 us -> 345 us
  matrix products: 127 us -> 33.1 us
  waiting for transfers between devices: 293 us -> 249 us
  starting transfers between devices: 22.6 us -> 13.8 us
    psum x1 -> x2, waiting for transfers between devices: 0.02 us -> 116 us  [the longest x1 92.4 us: local(): token_adapter = lax.psum(token_part.astype(jnp.bfloat16), ('ctx', 'tp'))]
    all_gather x1, waiting for transfers between devices: 198 us -> 83.7 us  [local(): lax.all_gather(output_cotangent, 'ctx', axis=0, tiled=True)]
    dot_general x36 -> x13, matrix products: 127 us -> 33.1 us  [the longest x1 9.39 us: local(): lax.dot_general(output_weight, whole_cotangent, (((1,), (1,)), ((), ())),...]
    all_to_all x5 -> x2, waiting for transfers between devices: 94.1 us -> 48.4 us  [the longest x1 48.4 us: local(): lax.all_to_all(jnp.stack([masked_filter, gated, outer_gate_proj]), 'ctx',...]
    all_gather x0 -> x1, blocking collectives: none -> 14.2 us  [local(): lax.all_gather(down_part.astype(jnp.bfloat16), 'ctx', axis=0, tiled=True)]
    all_to_all x5 -> x2, starting transfers between devices: 22.4 us -> 8.3 us  [the longest x1 4.6 us: local(): lax.all_to_all(jnp.stack([grad_gated_ch, outer_grad_ch]), 'ctx', split_ax...]
    psum x1 -> x0, blocking collectives: 10.5 us -> none  [local(): lax.psum(adapter_portion.astype(jnp.bfloat16), 'tp').astype(jnp.float32)]
    another operation x0 -> x3, local copies, waits for them, and re-layouts: none -> 5.61 us  [the longest x1 2.71 us: local(): jnp.stack([masked_filter, gated, outer_gate_proj])]
  transfers between devices with their start and end apart: 8 -> 7, of which waited for: 6 -> 4; matrix products, arithmetic and copies ran while one was open for 27% -> 7% of each run, Pallas kernels for 0% -> 0%
where the time goes in v1:
time: 345 us
  waiting for transfers between devices  249 us (72%)
  matrix products  33.1 us (10%)
  between operations  15.4 us (4%)
  blocking collectives  14.2 us (4%)
  starting transfers between devices  13.8 us (4%)
  local copies, waits for them, and re-layouts  12.5 us (4%)
  other arithmetic  6.46 us (2%)
    psum x1, waiting for transfers between devices, local(): token_adapter = lax.psum(token_part.astype(jnp.bfloat16), ('ctx', 'tp'))  92.4 us
    all_gather x1, waiting for transfers between devices, local(): lax.all_gather(output_cotangent, 'ctx', axis=0, tiled=True)  83.7 us
    all_to_all x1, waiting for transfers between devices, local(): lax.all_to_all(jnp.stack([masked_filter, gated, outer_gate_proj]), 'ctx',...  48.4 us
    psum x1, waiting for transfers between devices, local(): lax.psum(lax.dot_general(whole_cotangent, adapter_up_factor, (((1,), (1,)...  24.1 us
    all_gather x1, blocking collectives, local(): lax.all_gather(down_part.astype(jnp.bfloat16), 'ctx', axis=0, tiled=True)  14.2 us
    dot_general x1, matrix products, local(): lax.dot_general(output_weight, whole_cotangent, (((1,), (1,)), ((), ())),...  9.39 us
    dot_general x4, matrix products, dense_inverse(): lax.dot_general(spec, table, (((1,), (1,)), ((), ())), preferred_element_...  7.1 us
  transfers between devices with their start and end apart: 7, of which 4 were waited for; matrix products, arithmetic and copies ran while one was open for 7% of the time, Pallas kernels for 0%

profile of v1, /device:TPU:0, one launch (start us, length us, event | category | flops | bytes accessed | tf_op | source)
XLA Modules:
  0.0 344.7 jit_solution(15257451108282393221)
XLA Ops:
  8.0 0.0 copy-start
  8.0 0.0 all-gather.2.cloned.1.call-start
  8.1 0.7 all-gather.2.cloned.1.call-update
  8.7 0.0 reduce-scatter.2.cloned.1.call-start
  8.8 1.4 fusion.11
  10.2 83.7 %all-gather.2.cloned.1.call-done = bf16[1024,2048]{1,0:T(8,128)(2,1)} async-done(((bf16[256,2048]{1,0:T(8,128)(2,1)}), bf16[1024,2048]{1,0:T(8,128)(2,1)}) %all-gather.2.cloned.1.call-update) | async-done | bytes 4194320 | tf_op jit(solution)/shard_map/all_gather | solution.py:158
  93.9 9.4 %convolution_convert_fusion = bf16[1024,1024]{1,0:T(8,128)(2,1)} fusion(bf16[1024,2048]{1,0:T(8,128)(2,1)} %param.16, bf16[1024,2048]{1,0:T(8,128)(2,1)} %all-gather.2.cloned.1.call-done), kind=kOutput, calls=%fused_computation.1 | convolution fusion | flops 4296015872 | bytes 10485760 | tf_op jit(solution)/shard_map/dot_general | solution.py:170
  103.3 0.0 reduce-scatter.2.cloned.1.call-update
  103.3 1.0 copy-done.8
  104.3 0.2 copy-done.10
  104.5 0.1 fusion.13
  104.6 0.0 copy-done.13
  104.7 0.2 pad_maximum_fusion
  104.8 2.7 copy.21
  107.5 3.7 %all-to-all-start = ((bf16[3,1024,256]{2,0,1:T(4,128)(2,1)}), bf16[3,1024,256]{2,0,1:T(4,128)(2,1)S(1)}, u32[]{:S(2)}, u32[]{:S(2)}) async-start(bf16[3,1024,256]{2,0,1:T(4,128)(2,1)} %copy.21), calls=%async_computation | async-start | bytes 4194304 | tf_op jit(solution)/shard_map/all_to_all | solution.py:159
  111.2 0.0 all-reduce.3.cloned.1.call-start
  111.3 48.4 %all-to-all-done = bf16[3,1024,256]{2,0,1:T(4,128)(2,1)S(1)} async-done(((bf16[3,1024,256]{2,0,1:T(4,128)(2,1)}), bf16[3,1024,256]{2,0,1:T(4,128)(2,1)S(1)}, u32[]{:S(2)}, u32[]{:S(2)}) %all-to-all-start) | async-done | bytes 1572896 | tf_op jit(solution)/shard_map/all_to_all | solution.py:159
  159.7 1.5 copy.29
  161.1 0.0 copy-start.7
  161.2 1.5 slice_convert_fusion
  162.6 0.1 copy.27
  162.7 0.1 copy.25
  162.8 0.9 copy-done.7
  163.7 1.3 fusion.28
  165.0 0.0 copy-start.2
  165.0 0.0 copy-start.1
  165.0 1.3 fusion.29
  166.3 0.0 copy-done.2
  166.4 1.4 copy-done.12
  167.8 0.0 copy-done.1
  167.8 0.9 fusion.17
  168.7 0.0 reduce-scatter.2.cloned.1.call-done
  168.7 5.4 %collective-permute-start = (bf16[256,1024]{1,0:T(8,128)(2,1)}, bf16[256,1024]{1,0:T(8,128)(2,1)}, u32[]{:S(2)}, u32[]{:S(2)}) collective-permute-start(bf16[256,1024]{1,0:T(8,128)(2,1)} %reduce-scatter.2.cloned.1.call-done), channel_id=1, source_target_pairs={{0,0},{1,4},{2,8},{3,12},{4,1},{5,5},{6,9},{7,13},{8,2},{9,6},{10,... | collective-permute-start | bytes 1572872 | tf_op jit(solution)/shard_map/ppermute | solution.py:187
  174.1 0.0 copy-done
  174.1 4.2 %convolution_convert_fusion.2 = bf16[1024,32]{0,1:T(8,128)(2,1)} fusion(bf16[1024,2048]{1,0:T(8,128)(2,1)} %all-gather.2.cloned.1.call-done, bf16[32,2048]{1,0:T(8,128)(2,1)S(1)} %copy-done), kind=kOutput, calls=%fused_computation.18 | convolution fusion | flops 134250496 | bytes 4390912 | tf_op jit(solution)/shard_map/dot_general | solution.py:177
  178.2 0.0 all-reduce.3.cloned.1.call-update
  178.3 0.0 copy-start.6
  178.3 4.5 %fusion.3 = bf16[256,1024]{1,0:T(8,128)(2,1)} fusion(f32[256,1024]{1,0:T(8,128)S(1)} %fusion.17, bf16[1024,1024]{1,0:T(8,128)(2,1)} %constant.22, f32[256,2048]{1,0:T(8,128)} %copy-done.12, f32[256,2048]{1,0:T(8,128)} %copy-done.2), kind=kOutput, calls=%fused_computation.15 | convolution fusion | flops 538705920 | bytes 7864320 | tf_op jit(solution)/shard_map/dot_general | solution.py:112
  182.8 0.2 copy.26
  183.0 24.1 %all-reduce.3.cloned.1.call-done = bf16[1024,32]{0,1:T(8,128)(2,1)} async-done(((bf16[1024,32]{0,1:T(8,128)(2,1)}), bf16[1024,32]{0,1:T(8,128)(2,1)}) %all-reduce.3.cloned.1.call-update) | async-done | bytes 65552 | tf_op jit(solution)/shard_map/psum | solution.py:176
  207.1 0.0 collective-permute-done
  207.1 1.4 add_convert_fusion.2
  208.5 1.2 fusion.12
  209.8 3.6 %fusion.14 = f32[256,2048]{1,0:T(8,128)S(1)} fusion(bf16[1024,2048]{1,0:T(8,128)(2,1)} %constant.20.clone, f32[256,1024]{1,0:T(8,128)S(1)} %bitcast.46, bf16[256,1024]{1,0:T(8,128)(2,1)S(1)} %add_convert_fusion.2), kind=kOutput, calls=%fused_computation.37 | convolution fusion | flops 1074528256 | bytes 7864320 | tf_op jit(solution)/shard_map/dot_general | solution.py:106
  213.4 0.0 copy-start.5
  213.4 0.9 fusion.16
  214.3 0.7 copy-done.5
  215.0 0.8 fusion.4
  215.8 0.1 pad_maximum_fusion.1
  215.9 0.0 copy-start.4
  215.9 2.0 copy.23
  218.0 4.6 %all-to-all-start.1 = ((bf16[2,256,1024]{1,0,2:T(2,128)(2,1)}), bf16[2,256,1024]{1,0,2:T(2,128)(2,1)S(1)}, u32[]{:S(2)}, u32[]{:S(2)}) async-start(bf16[2,256,1024]{1,0,2:T(2,128)(2,1)} %copy.23), calls=%async_computation.2 | async-start | bytes 2097152 | tf_op jit(solution)/shard_map/all_to_all | solution.py:209
  222.6 0.8 convolution_convert_fusion.1
  223.4 0.0 all-reduce.5.cloned.1.call-update
  223.4 92.4 %all-reduce.5.cloned.1.call-done = bf16[1024,32]{0,1:T(8,128)(2,1)} async-done(((bf16[1024,32]{0,1:T(8,128)(2,1)}), bf16[1024,32]{0,1:T(8,128)(2,1)}) %all-reduce.5.cloned.1.call-update) | async-done | bytes 65552 | tf_op jit(solution)/shard_map/psum | solution.py:207
  315.8 3.8 %convolution_multiply_fusion = f32[32,2048]{1,0:T(8,128)} fusion(bf16[1024,32]{0,1:T(8,128)(2,1)} %all-reduce.5.cloned.1.call-done, bf16[1024,2048]{1,0:T(8,128)(2,1)} %all-gather.2.cloned.1.call-done), kind=kOutput, calls=%fused_computation | convolution fusion | flops 134283264 | bytes 4521984 | tf_op jit(solution)/shard_map/dot_general | solution.py:218
  319.6 0.3 convolution_convert_fusion.3
  319.8 14.2 %all_gather.7 = bf16[1024,32]{0,1:T(8,128)(2,1)S(1)} all-gather(bf16[256,32]{0,1:T(8,128)(2,1)S(1)} %convolution_convert_fusion.3), channel_id=1, replica_groups=mesh['groups'=2,'ctx'=4,'tp'=4] {'ctx'}, dimensions={0}, use_global_device_ids=true | all-gather | bytes 81920 | tf_op jit(solution)/shard_map/all_gather | solution.py:217
  334.0 0.7 convert_multiply_fusion.6
  334.7 0.0 all-to-all-done.1
  334.7 0.7 copy.24
  335.4 0.9 fusion.27
  336.3 0.0 copy-done.11
  336.3 1.2 fusion.10
  (17 shorter events, 0.0 us)
Async XLA Ops:
  8.0 166.1 %copy-start = (bf16[32,2048]{1,0:T(8,128)(2,1)S(1)}, bf16[32,2048]{1,0:T(8,128)(2,1)}, u32[]{:S(2)}) copy-start(bf16[32,2048]{1,0:T(8,128)(2,1)} %param.18) | copy-start | bytes 393220
  8.0 85.9 %all-gather.2.cloned.1.call-start = ((), (), s32[]{:S(2)}) async-start(), calls=%async_computation.3 | async-start | bytes 5242880 | tf_op jit(solution)/shard_map/all_gather | solution.py:158
  8.7 159.9 %reduce-scatter.2.cloned.1.call-start = ((), (), s32[]{:S(2)}) async-start(), calls=%async_computation.4 | async-start | bytes 2621440 | tf_op jit(solution)/shard_map/reduce_scatter | solution.py:185
  103.3 1.0 copy-start.8
  103.3 1.2 copy-start.10
  103.3 1.4 copy-start.13
  107.5 52.1 %all-to-all-start = ((bf16[3,1024,256]{2,0,1:T(4,128)(2,1)}), bf16[3,1024,256]{2,0,1:T(4,128)(2,1)S(1)}, u32[]{:S(2)}, u32[]{:S(2)}) async-start(bf16[3,1024,256]{2,0,1:T(4,128)(2,1)} %copy.21), calls=%async_computation | async-start | bytes 4194304 | tf_op jit(solution)/shard_map/all_to_all | solution.py:159
  111.2 95.8 %all-reduce.3.cloned.1.call-start = ((), (), s32[]{:S(2)}) async-start(), calls=%async_computation.5 | async-start | bytes 131072 | tf_op jit(solution)/shard_map/psum | solution.py:176
  161.1 2.6 copy-start.7
  165.0 1.4 copy-start.2
  165.0 2.7 copy-start.1
  166.4 1.4 copy-start.12
  168.7 38.4 %collective-permute-start = (bf16[256,1024]{1,0:T(8,128)(2,1)}, bf16[256,1024]{1,0:T(8,128)(2,1)}, u32[]{:S(2)}, u32[]{:S(2)}) collective-permute-start(bf16[256,1024]{1,0:T(8,128)(2,1)} %reduce-scatter.2.cloned.1.call-done), channel_id=1, source_target_pairs={{0,0},{1,4},{2,8},{3,12},{4,1},{5,5},{6,9},{7,13},{8,2},{9,6},{10,... | collective-permute-start | bytes 1572872 | tf_op jit(solution)/shard_map/ppermute | solution.py:187
  178.3 4.5 %copy-start.6 = (f32[1,256,4,256]{3,2,1,0:T(4,128)S(1)}, f32[1,256,4,256]{3,2,1,0:T(4,128)}, u32[]{:S(2)}) copy-start(f32[1,256,4,256]{3,2,1,0:T(4,128)} %get-tuple-element.5) | copy-start | bytes 3145732
  182.8 24.3 %copy-start.15 = (bf16[1024,32]{0,1:T(8,128)(2,1)S(1)}, bf16[1024,32]{0,1:T(8,128)(2,1)}, u32[]{:S(2)}) copy-start(bf16[1024,32]{0,1:T(8,128)(2,1)} %param.17) | copy-start | bytes 196612
  209.8 3.6 %copy-start.3 = (f32[256,2048]{1,0:T(8,128)S(1)}, f32[256,2048]{1,0:T(8,128)}, u32[]{:S(2)}) copy-start(f32[256,2048]{1,0:T(8,128)} %copy-done.2) | copy-start | bytes 6291460
  213.4 1.6 copy-start.5
  215.9 6.7 %copy-start.4 = (bf16[256,1024]{1,0:T(8,128)(2,1)S(1)}, bf16[256,1024]{1,0:T(8,128)(2,1)}, u32[]{:S(2)}) copy-start(bf16[256,1024]{1,0:T(8,128)(2,1)} %fusion.3) | copy-start | bytes 1572868
  218.0 116.7 %all-to-all-start.1 = ((bf16[2,256,1024]{1,0,2:T(2,128)(2,1)}), bf16[2,256,1024]{1,0,2:T(2,128)(2,1)S(1)}, u32[]{:S(2)}, u32[]{:S(2)}) async-start(bf16[2,256,1024]{1,0,2:T(2,128)(2,1)} %copy.23), calls=%async_computation.2 | async-start | bytes 2097152 | tf_op jit(solution)/shard_map/all_to_all | solution.py:209
  222.6 93.3 %all-reduce.5.cloned.1.call-start = ((), (), s32[]{:S(2)}) async-start(), calls=%async_computation.6 | async-start | bytes 131072 | tf_op jit(solution)/shard_map/psum | solution.py:207
  223.4 96.2 %copy-start.14 = (bf16[1024,32]{0,1:T(8,128)(2,1)S(1)}, bf16[1024,32]{0,1:T(8,128)(2,1)}, u32[]{:S(2)}) copy-start(bf16[1024,32]{0,1:T(8,128)(2,1)} %all-reduce.3.cloned.1.call-done) | copy-start | bytes 196612
  334.7 1.6 copy-start.9
  334.7 1.6 copy-start.11
Sparse Core Ops, SparseCore 0:
  10.4 83.4 all-gather.1
  103.5 29.9 reduce-scatter.1
  178.4 28.6 all-reduce.2
Sparse Core Ops, SparseCore 1:
  227.1 88.7 all-reduce.4

commit v2 on v1

--- a/solution.py
+++ b/solution.py
@@ -1,3 +1,4 @@
+import functools
 import math
 
 import jax
@@ -5,6 +6,8 @@
 import ml_dtypes
 import numpy as np
 from jax import lax
+from jax.experimental import pallas as pl
+from jax.experimental.pallas import tpu as pltpu
 from jax.sharding import PartitionSpec as P
 
 adapter_scale = 2.0
@@ -131,6 +134,178 @@
         table,
     )
     return conv, back
+
+
+kernel_peers = 16
+
+
+def position():
+    ctx_size, tp_size = lax.axis_size("ctx"), lax.axis_size("tp")
+    count = ctx_size * tp_size
+    me = lax.axis_index("ctx") * tp_size + lax.axis_index("tp")
+
+    def peer(step):
+        other = lax.rem(me + step, count)
+        return {"ctx": other // tp_size, "tp": lax.rem(other, tp_size)}
+
+    return me, count, peer
+
+
+def greet(count, peer):
+    barrier = pltpu.get_barrier_semaphore()
+    for step in range(1, count):
+        pl.semaphore_signal(
+            barrier, inc=1, device_id=peer(step), device_id_type=pl.DeviceIdType.MESH
+        )
+    pl.semaphore_wait(barrier, count - 1)
+
+
+def push(src, dst, send_sem, recv_sem, device):
+    copy = pltpu.make_async_remote_copy(
+        src_ref=src,
+        dst_ref=dst,
+        send_sem=send_sem,
+        recv_sem=recv_sem,
+        device_id=device,
+        device_id_type=pl.DeviceIdType.MESH,
+    )
+    copy.start()
+    return copy
+
+
+def return_kernel(
+    ctx_size,
+    tp_size,
+    grad_ref,
+    outer_ref,
+    token_ref,
+    down_ref,
+    cotangent_ref,
+    grad_out,
+    outer_out,
+    down_out,
+    up_out,
+    parts,
+    whole,
+    send_tok,
+    recv_tok,
+    send_all,
+    recv_all,
+    send_row,
+    recv_row,
+    local_sem,
+):
+    me, count, peer = position()
+    ctx, tp = lax.axis_index("ctx"), lax.axis_index("tp")
+    rows, length = grad_ref.shape
+    width = length // ctx_size
+    lanes = length // 128
+    greet(count, peer)
+
+    def chunk(ref, place):
+        top = pl.multiple_of(place // lanes * 16, 16)
+        left = pl.multiple_of(lax.rem(place, lanes) * 128, 128)
+        return ref.at[pl.ds(top, 16), pl.ds(left, 128)]
+
+    copies = []
+    for step in range(1, count):
+        copies.append(
+            push(
+                chunk(token_ref, lax.rem(me + step, count)),
+                parts.at[step],
+                send_tok.at[step],
+                recv_tok.at[step],
+                peer(step),
+            )
+        )
+    my_rows = pl.ds(pl.multiple_of(ctx * rows, 16), rows)
+    my_cols = pl.ds(pl.multiple_of(ctx * width, 128), width)
+    my_lags = pl.ds(pl.multiple_of(ctx * rows, 128), rows)
+    later = []
+    for step in range(1, ctx_size):
+        other = lax.rem(ctx + step, ctx_size)
+        device = {"ctx": other, "tp": tp}
+        cols = pl.ds(pl.multiple_of(other * width, 128), width)
+        moves = (
+            (down_ref, down_out.at[:, my_lags]),
+            (grad_ref.at[:, cols], grad_out.at[my_rows, :]),
+            (outer_ref.at[:, cols], outer_out.at[my_rows, :]),
+        )
+        for kind, (src, dst) in enumerate(moves):
+            later.append(push(src, dst, send_row.at[kind, step], recv_row.at[kind, step], device))
+    down_out[:, my_lags] = down_ref[...]
+    grad_out[my_rows, :] = grad_ref[:, my_cols]
+    outer_out[my_rows, :] = outer_ref[:, my_cols]
+
+    own = pltpu.make_async_copy(chunk(token_ref, me), parts.at[0], local_sem)
+    own.start()
+    own.wait()
+    total = parts[0].astype(jnp.float32)
+    for step in range(1, count):
+        copies[step - 1].wait_recv()
+        total += parts[step].astype(jnp.float32)
+    for copy in copies:
+        copy.wait_send()
+    parts[0] = total.astype(jnp.bfloat16)
+    copies = []
+    for step in range(1, count):
+        copies.append(
+            push(
+                parts.at[0],
+                chunk(whole, me),
+                send_all.at[step],
+                recv_all.at[step],
+                peer(step),
+            )
+        )
+    own = pltpu.make_async_copy(parts.at[0], chunk(whole, me), local_sem)
+    own.start()
+    own.wait()
+    for copy in copies:
+        copy.wait()
+    up_out[...] = adapter_scale * jnp.dot(
+        whole[...], cotangent_ref[...], preferred_element_type=jnp.float32
+    )
+    for copy in later:
+        copy.wait()
+
+
+def return_all(grad_gated_ch, outer_grad_ch, token_t, down_t, whole_cotangent):
+    ctx_size, tp_size = lax.axis_size("ctx"), lax.axis_size("tp")
+    count = ctx_size * tp_size
+    rows, length = grad_gated_ch.shape
+    rank = token_t.shape[0]
+    tokens = jax.ShapeDtypeStruct((rows * ctx_size, length // ctx_size), jnp.bfloat16)
+    dma = pltpu.SemaphoreType.DMA
+    return pl.pallas_call(
+        functools.partial(return_kernel, ctx_size, tp_size),
+        out_shape=(
+            tokens,
+            tokens,
+            jax.ShapeDtypeStruct((rank, rows * ctx_size), jnp.bfloat16),
+            jax.ShapeDtypeStruct((rank, whole_cotangent.shape[1]), jnp.float32),
+        ),
+        in_specs=[pl.BlockSpec(memory_space=pltpu.VMEM)] * 5,
+        out_specs=(pl.BlockSpec(memory_space=pltpu.VMEM),) * 4,
+        scratch_shapes=[
+            pltpu.VMEM((count, 16, 128), jnp.bfloat16),
+            pltpu.VMEM((rank, length), jnp.bfloat16),
+            dma((count,)),
+            dma((count,)),
+            dma((count,)),
+            dma((count,)),
+            dma((3, ctx_size)),
+            dma((3, ctx_size)),
+            dma,
+        ],
+        compiler_params=pltpu.CompilerParams(
+            collective_id=1, has_side_effects=True, vmem_limit_bytes=40 << 20
+        ),
+    )(grad_gated_ch, outer_grad_ch, token_t, down_t, whole_cotangent)
+
+
+def token_by_kernel(count, shape, rank):
+    return count <= kernel_peers and shape[1] <= dense_length and rank * shape[1] == count * 2048
 
 
 def local(
@@ -198,6 +373,30 @@
     else:
         conv_ch, grad_gated_ch = convolve(filter_ch.astype(jnp.float32), gated_ch, grad_conv)
     block_output = product_bf(outer_ch, conv_ch)
+    outer_grad_ch = product_bf(projected_gradient, conv_ch)
+    if token_by_kernel(ctx_size * tp_size, filter_ch.shape, adapter_down_factor.shape[1]):
+        token_t = lax.dot_general(
+            down_rows,
+            block_output,
+            (((0,), (0,)), ((), ())),
+            preferred_element_type=jnp.float32,
+        ).astype(jnp.bfloat16)
+        down_t = lax.dot_general(
+            adapter_backward,
+            block_output,
+            (((0,), (1,)), ((), ())),
+            preferred_element_type=jnp.float32,
+        ).astype(jnp.bfloat16)
+        grad_gated, outer_gate_gradient, down_sum, up_sum = return_all(
+            grad_gated_ch, outer_grad_ch, token_t, down_t, whole_cotangent
+        )
+        return (
+            product_bf(grad_gated, value_projection),
+            outer_gate_gradient,
+            product_bf(grad_gated, inner_gate_proj),
+            down_sum.astype(jnp.float32).T * adapter_scale,
+            up_sum,
+        )
     token_part = lax.dot_general(
         block_output,
         down_rows,
@@ -205,7 +404,6 @@
         preferred_element_type=jnp.float32,
     )
     token_adapter = lax.psum(token_part.astype(jnp.bfloat16), ("ctx", "tp"))
-    outer_grad_ch = product_bf(projected_gradient, conv_ch)
     grad_gated, outer_gate_gradient = lax.all_to_all(
         jnp.stack([grad_gated_ch, outer_grad_ch]),
         "ctx",

time: 345 us -> 262 us (0.76)
  waiting for transfers between devices: 249 us -> 159 us
  Pallas kernels: 0 us -> 33.8 us
  blocking collectives: 14.2 us -> 0 us
  starting transfers between devices: 13.8 us -> 9.27 us
    psum x1 -> x0, waiting for transfers between devices: 92.4 us -> none  [local(): token_adapter = lax.psum(token_part.astype(jnp.bfloat16), ('ctx', 'tp'))]
    pallas_call x0 -> x1, Pallas kernels: none -> 33.8 us  [return_all(): pl.pallas_call(functools.partial(return_kernel, ctx_size, tp_size), out_s...]
    all_gather x1 -> x0, blocking collectives: 14.2 us -> none  [local(): lax.all_gather(down_part.astype(jnp.bfloat16), 'ctx', axis=0, tiled=True)]
    all_to_all x1 -> x0, starting transfers between devices: 4.6 us -> none  [local(): lax.all_to_all(jnp.stack([grad_gated_ch, outer_grad_ch]), 'ctx', split_ax...]
    dot_general x3 -> x2, matrix products: 4.86 us -> 0.46 us  [the longest x1 0.26 us: local(): lax.dot_general(adapter_backward, block_output, (((0,), (1,)), ((), ())),...]
    unnamed x35 -> x41, local copies, waits for them, and re-layouts: 4.66 us -> 6.93 us
  transfers between devices with their start and end apart: 7 -> 5, of which waited for: 4 -> 3; matrix products, arithmetic and copies ran while one was open for 7% -> 8% of each run, Pallas kernels for 0% -> 0%
where the time goes in v2:
time: 262 us
  waiting for transfers between devices  159 us (61%)
  Pallas kernels  33.8 us (13%)
  matrix products  30.9 us (12%)
  between operations  14 us (5%)
  local copies, waits for them, and re-layouts  11.1 us (4%)
  starting transfers between devices  9.27 us (4%)
  other arithmetic  3.85 us (1%)
    all_gather x1, waiting for transfers between devices, local(): lax.all_gather(output_cotangent, 'ctx', axis=0, tiled=True)  85.1 us
    all_to_all x1, waiting for transfers between devices, local(): lax.all_to_all(jnp.stack([masked_filter, gated, outer_gate_proj]), 'ctx',...  48.4 us
    pallas_call x1, Pallas kernels, return_all(): pl.pallas_call(functools.partial(return_kernel, ctx_size, tp_size), out_s...  33.8 us
    psum x1, waiting for transfers between devices, local(): lax.psum(lax.dot_general(whole_cotangent, adapter_up_factor, (((1,), (1,)...  24.5 us
    dot_general x1, matrix products, local(): lax.dot_general(output_weight, whole_cotangent, (((1,), (1,)), ((), ())),...  9.39 us
    dot_general x3, matrix products, dense_spectrum(): spec = jnp.dot(field, table, preferred_element_type=jnp.float32)  8.89 us
    unnamed x41, local copies, waits for them, and re-layouts  6.93 us
    dot_general x4, matrix products, dense_inverse(): lax.dot_general(spec, table, (((1,), (1,)), ((), ())), preferred_element_...  6.6 us
  transfers between devices with their start and end apart: 5, of which 3 were waited for; matrix products, arithmetic and copies ran while one was open for 8% of the time, Pallas kernels for 0%

profile of v2, /device:TPU:0, one launch (start us, length us, event | category | flops | bytes accessed | tf_op | source)
XLA Modules:
  0.0 261.6 jit_solution(10569377461347968041)
XLA Ops:
  7.2 0.0 copy-start
  7.2 0.0 all-gather.2.cloned.1.call-start
  7.2 0.7 all-gather.2.cloned.1.call-update
  7.9 0.0 reduce-scatter.2.cloned.1.call-start
  8.0 85.1 %all-gather.2.cloned.1.call-done.cotangent_ref = bf16[1024,2048]{1,0:T(8,128)(2,1)} async-done(((bf16[256,2048]{1,0:T(8,128)(2,1)}), bf16[1024,2048]{1,0:T(8,128)(2,1)}) %all-gather.2.cloned.1.call-update) | async-done | bytes 4194320 | tf_op jit(solution)/shard_map/all_gather | solution.py:333
  93.1 9.4 %convolution_convert_fusion = bf16[1024,1024]{1,0:T(8,128)(2,1)} fusion(bf16[1024,2048]{1,0:T(8,128)(2,1)} %param.16, bf16[1024,2048]{1,0:T(8,128)(2,1)} %all-gather.2.cloned.1.call-done.cotangent_ref), kind=kOutput, calls=%fused_computation | convolution fusion | flops 4296015872 | bytes 10485760 | tf_op jit(solution)/shard_map/dot_general | solution.py:345
  102.5 0.0 copy-start.8
  102.5 0.0 copy-start.10
  102.5 0.0 reduce-scatter.2.cloned.1.call-update
  102.5 0.0 copy-start.14
  102.5 1.0 copy-done.8
  103.5 0.2 copy-done.10
  103.7 0.1 fusion.11
  103.8 0.2 copy-done.13
  104.0 0.0 copy-done.17
  104.0 0.2 fusion.10
  104.2 0.0 copy-done.14
  104.2 0.2 pad_maximum_fusion
  104.4 2.7 %copy.16 = bf16[3,1024,256]{2,0,1:T(4,128)(2,1)} copy(bf16[3,1024,256]{2,1,0:T(8,128)(2,1)S(1)} %pad_maximum_fusion) | data formatting | bytes 3145728 | tf_op jit(solution)/shard_map/stack | solution.py:335
  107.1 3.7 %all-to-all-start = ((bf16[3,1024,256]{2,0,1:T(4,128)(2,1)}), bf16[3,1024,256]{2,0,1:T(4,128)(2,1)S(1)}, u32[]{:S(2)}, u32[]{:S(2)}) async-start(bf16[3,1024,256]{2,0,1:T(4,128)(2,1)} %copy.16), calls=%async_computation | async-start | bytes 4194304 | tf_op jit(solution)/shard_map/all_to_all | solution.py:334
  110.8 0.0 all-reduce.2.cloned.1.call-start
  110.8 48.4 %all-to-all-done = bf16[3,1024,256]{2,0,1:T(4,128)(2,1)S(1)} async-done(((bf16[3,1024,256]{2,0,1:T(4,128)(2,1)}), bf16[3,1024,256]{2,0,1:T(4,128)(2,1)S(1)}, u32[]{:S(2)}, u32[]{:S(2)}) %all-to-all-start) | async-done | bytes 1572896 | tf_op jit(solution)/shard_map/all_to_all | solution.py:334
  159.2 1.5 copy.22
  160.7 0.0 copy-start.7
  160.7 1.5 fusion.25
  162.2 0.1 copy.18
  162.3 0.1 copy.20
  162.4 0.9 copy-done.7
  163.3 2.7 %fusion.26 = f32[256,2048]{1,0:T(8,128)} fusion(bf16[256,1024]{1,0:T(8,128)(2,1)S(1)} %bitcast.43, bf16[1024,2048]{1,0:T(8,128)(2,1)S(1)} %copy-done.7), kind=kOutput, calls=%fused_computation.44 | convolution fusion | flops 1073741824 | bytes 6815744 | tf_op jit(solution)/shard_map/dot_general | solution.py:109
  166.0 2.6 %fusion.27 = f32[256,2048]{1,0:T(8,128)} fusion(bf16[256,1024]{1,0:T(8,128)(2,1)S(1)} %bitcast.44, bf16[1024,2048]{1,0:T(8,128)(2,1)S(1)} %copy-done.7), kind=kOutput, calls=%fused_computation.45 | convolution fusion | flops 1073741824 | bytes 6815744 | tf_op jit(solution)/shard_map/dot_general | solution.py:109
  168.6 5.5 %collective-permute-start = (bf16[256,1024]{1,0:T(8,128)(2,1)}, bf16[256,1024]{1,0:T(8,128)(2,1)}, u32[]{:S(2)}, u32[]{:S(2)}) collective-permute-start(bf16[256,1024]{1,0:T(8,128)(2,1)} %reduce-scatter.2.cloned.1.call-done), channel_id=1, source_target_pairs={{0,0},{1,4},{2,8},{3,12},{4,1},{5,5},{6,9},{7,13},{8,2},{9,6},{10,... | collective-permute-start | bytes 1572872 | tf_op jit(solution)/shard_map/ppermute | solution.py:362
  174.1 0.0 copy-done
  174.1 4.2 %convolution_convert_fusion.2 = bf16[1024,32]{0,1:T(8,128)(2,1)} fusion(bf16[1024,2048]{1,0:T(8,128)(2,1)} %all-gather.2.cloned.1.call-done.cotangent_ref, bf16[32,2048]{1,0:T(8,128)(2,1)S(1)} %copy-done), kind=kOutput, calls=%fused_computation.16 | convolution fusion | flops 134250496 | bytes 4390912 | tf_op jit(solution)/shard_map/dot_general | solution.py:352
  178.2 0.0 all-reduce.2.cloned.1.call-update
  178.3 0.0 copy-done.2
  178.3 0.0 copy-start.5
  178.3 4.1 %fusion.15 = f32[256,1024]{1,0:T(8,128)} fusion(bf16[1024,1024]{1,0:T(8,128)(2,1)S(1)} %copy-done.2, f32[256,2048]{1,0:T(8,128)} %fusion.27, f32[256,2048]{1,0:T(8,128)} %fusion.26), kind=kOutput, calls=%fused_computation.35 | convolution fusion | flops 537919488 | bytes 7340032 | tf_op jit(solution)/shard_map/dot_general | solution.py:115
  182.4 0.0 copy-done.5
  182.4 0.2 copy.19
  182.6 24.5 %all-reduce.2.cloned.1.call-done = bf16[1024,32]{0,1:T(8,128)(2,1)} async-done(((bf16[1024,32]{0,1:T(8,128)(2,1)}), bf16[1024,32]{0,1:T(8,128)(2,1)}) %all-reduce.2.cloned.1.call-update) | async-done | bytes 65552 | tf_op jit(solution)/shard_map/psum | solution.py:351
  207.1 0.0 collective-permute-done
  207.1 0.0 copy-done.16
  207.1 1.4 add_convert_fusion.2
  208.5 0.0 copy-start.3
  208.5 3.6 %fusion.12 = f32[256,2048]{1,0:T(8,128)S(1)} fusion(bf16[1024,2048]{1,0:T(8,128)(2,1)} %constant.19.clone, f32[256,1024]{1,0:T(8,128)S(1)} %bitcast.35, bf16[256,1024]{1,0:T(8,128)(2,1)S(1)} %add_convert_fusion.2), kind=kOutput, calls=%fused_computation.33 | convolution fusion | flops 1074528256 | bytes 7864320 | tf_op jit(solution)/shard_map/dot_general | solution.py:109
  212.1 0.0 copy-done.3
  212.1 0.0 copy-start.4
  212.2 0.8 fusion.14
  213.0 0.8 copy-done.4
  213.7 0.8 fusion.2.grad_ref
  214.6 0.4 copy-done.6
  215.0 0.7 copy-done.12
  215.7 0.9 fusion.6
  216.5 0.2 convolution_convert_fusion.1.token_ref
  216.7 0.0 copy-done.15
  216.8 0.3 convolution_convert_fusion.3.down_ref
  217.0 0.9 copy-done.1
  217.9 33.8 %shard_map.137 = (bf16[1024,256]{1,0:T(8,128)(2,1)S(1)}, bf16[1024,256]{1,0:T(8,128)(2,1)S(1)}, bf16[32,1024]{1,0:T(8,128)(2,1)S(1)}, f32[32,2048]{1,0:T(8,128)S(1)}) custom-call(bf16[256,1024]{1,0:T(8,128)(2,1)S(1)} %fusion.2.grad_ref, bf16[256,1024]{1,0:T(8,128)(2,1)S(1)} %get-tuple-element.18.outer_ref, ...), custom_call_target="tpu_custom_call" | custom-call | tf_op jit(solution)/shard_map/pallas_call | solution.py:280
  251.7 0.0 copy-done.9
  251.7 0.0 copy-done.11
  251.7 1.2 fusion.9
  252.9 0.7 multiply_bitcast_fusion
  253.6 0.8 copy.26
  254.4 0.7 copy.27
  (12 shorter events, 0.0 us)
Async XLA Ops:
  7.2 166.9 %copy-start = (bf16[32,2048]{1,0:T(8,128)(2,1)S(1)}, bf16[32,2048]{1,0:T(8,128)(2,1)}, u32[]{:S(2)}) copy-start(bf16[32,2048]{1,0:T(8,128)(2,1)} %param.18) | copy-start | bytes 393220
  7.2 85.9 %all-gather.2.cloned.1.call-start = ((), (), s32[]{:S(2)}) async-start(), calls=%async_computation.2 | async-start | bytes 5242880 | tf_op jit(solution)/shard_map/all_gather | solution.py:333
  7.9 160.7 %reduce-scatter.2.cloned.1.call-start = ((), (), s32[]{:S(2)}) async-start(), calls=%async_computation.3 | async-start | bytes 2621440 | tf_op jit(solution)/shard_map/reduce_scatter | solution.py:360
  102.5 1.0 copy-start.8
  102.5 1.2 copy-start.10
  102.5 1.5 copy-start.13
  102.5 1.5 copy-start.17
  102.5 1.7 copy-start.14
  107.1 52.1 %all-to-all-start = ((bf16[3,1024,256]{2,0,1:T(4,128)(2,1)}), bf16[3,1024,256]{2,0,1:T(4,128)(2,1)S(1)}, u32[]{:S(2)}, u32[]{:S(2)}) async-start(bf16[3,1024,256]{2,0,1:T(4,128)(2,1)} %copy.16), calls=%async_computation | async-start | bytes 4194304 | tf_op jit(solution)/shard_map/all_to_all | solution.py:334
  110.8 96.3 %all-reduce.2.cloned.1.call-start = ((), (), s32[]{:S(2)}) async-start(), calls=%async_computation.4 | async-start | bytes 131072 | tf_op jit(solution)/shard_map/psum | solution.py:351
  160.7 2.6 copy-start.7
  168.6 9.7 %copy-start.2 = (bf16[1024,1024]{1,0:T(8,128)(2,1)S(1)}, bf16[1024,1024]{1,0:T(8,128)(2,1)}, u32[]{:S(2)}) copy-start(bf16[1024,1024]{1,0:T(8,128)(2,1)} %constant.20) | copy-start | bytes 6291460
  168.6 38.5 %collective-permute-start = (bf16[256,1024]{1,0:T(8,128)(2,1)}, bf16[256,1024]{1,0:T(8,128)(2,1)}, u32[]{:S(2)}, u32[]{:S(2)}) collective-permute-start(bf16[256,1024]{1,0:T(8,128)(2,1)} %reduce-scatter.2.cloned.1.call-done), channel_id=1, source_target_pairs={{0,0},{1,4},{2,8},{3,12},{4,1},{5,5},{6,9},{7,13},{8,2},{9,6},{10,... | collective-permute-start | bytes 1572872 | tf_op jit(solution)/shard_map/ppermute | solution.py:362
  178.3 4.1 %copy-start.5 = (f32[1,256,4,256]{3,2,1,0:T(4,128)S(1)}, f32[1,256,4,256]{3,2,1,0:T(4,128)}, u32[]{:S(2)}) copy-start(f32[1,256,4,256]{3,2,1,0:T(4,128)} %get-tuple-element.14) | copy-start | bytes 3145732
  182.4 24.7 %copy-start.16 = (bf16[1024,32]{0,1:T(8,128)(2,1)S(1)}, bf16[1024,32]{0,1:T(8,128)(2,1)}, u32[]{:S(2)}) copy-start(bf16[1024,32]{0,1:T(8,128)(2,1)} %param.17) | copy-start | bytes 196612
  208.5 3.6 %copy-start.3 = (f32[256,2048]{1,0:T(8,128)S(1)}, f32[256,2048]{1,0:T(8,128)}, u32[]{:S(2)}) copy-start(f32[256,2048]{1,0:T(8,128)} %fusion.26) | copy-start | bytes 6291460
  212.1 1.6 copy-start.4
  213.7 1.2 copy-start.6
  213.7 1.9 copy-start.12
  215.7 1.1 copy-start.15
  215.7 2.2 copy-start.1
  217.9 33.8 %copy-start.9 = (bf16[1024,256]{1,0:T(8,128)(2,1)S(1)}, bf16[1024,256]{1,0:T(8,128)(2,1)}, u32[]{:S(2)}) copy-start(bf16[1024,256]{1,0:T(8,128)(2,1)} %param.10) | copy-start | bytes 1572868
  217.9 33.8 %copy-start.11 = (bf16[1024,256]{1,0:T(8,128)(2,1)S(1)}, bf16[1024,256]{1,0:T(8,128)(2,1)}, u32[]{:S(2)}) copy-start(bf16[1024,256]{1,0:T(8,128)(2,1)} %param.12) | copy-start | bytes 1572868
Sparse Core Ops, SparseCore 0:
  9.6 83.4 all-gather.1
  102.6 29.9 reduce-scatter.1
  178.4 28.6 all-reduce.1

commit v3 on v2

--- a/solution.py
+++ b/solution.py
@@ -304,6 +304,289 @@
     )(grad_gated_ch, outer_grad_ch, token_t, down_t, whole_cotangent)
 
 
+exchange_step = 3
+
+
+def project_kernel(
+    ctx_size,
+    tp_size,
+    cotangent_ref,
+    weight_ref,
+    up_ref,
+    filter_ref,
+    gated_ref,
+    outer_ref,
+    whole_out,
+    filter_out,
+    gated_out,
+    outer_out,
+    back_out,
+    adapter_out,
+    partial,
+    landed,
+    summed,
+    adapter_parts,
+    adapter_sum,
+    send_relay,
+    recv_relay,
+    send_part,
+    recv_part,
+    send_sum,
+    recv_sum,
+    send_row,
+    recv_row,
+    send_ad,
+    recv_ad,
+    send_adsum,
+    recv_adsum,
+):
+    me, count, peer = position()
+    ctx, tp = lax.axis_index("ctx"), lax.axis_index("tp")
+    width = cotangent_ref.shape[0]
+    rows = weight_ref.shape[0] // tp_size
+    ch_rows = filter_out.shape[0]
+    steps = 2 * (ctx_size - 1) + 1
+    greet(count, peer)
+
+    def describe(src, dst, send_sem, recv_sem, device):
+        return pltpu.make_async_remote_copy(
+            src_ref=src,
+            dst_ref=dst,
+            send_sem=send_sem,
+            recv_sem=recv_sem,
+            device_id=device,
+            device_id_type=pl.DeviceIdType.MESH,
+        )
+
+    def token_rows(block):
+        return pl.ds(pl.multiple_of(block * width, 128), width)
+
+    def stage(i):
+        hop = (i + 1) // 2
+        odd = lax.rem(i, 2)
+        block = ctx + hop - 2 * odd * hop
+        return hop, 1 - odd, block, jnp.logical_and(block >= 0, block < ctx_size)
+
+    def relay(way, hop, block):
+        target = lax.rem(ctx + ctx_size + 1 - 2 * way, ctx_size)
+        held = whole_out.at[token_rows(block), :]
+        return describe(
+            held,
+            held,
+            send_relay.at[way, hop],
+            recv_relay.at[way, hop + 1],
+            {"ctx": target, "tp": tp},
+        )
+
+    def can_relay(way):
+        target = ctx + 1 - 2 * way
+        return jnp.logical_and(target >= 0, target < ctx_size)
+
+    whole_out[token_rows(ctx), :] = cotangent_ref[...]
+    for way in range(2):
+        pl.when(can_relay(way))(lambda way=way: relay(way, 0, ctx).start())
+
+    adapter_parts[0] = lax.dot_general(
+        up_ref[...],
+        cotangent_ref[...],
+        (((1,), (1,)), ((), ())),
+        preferred_element_type=jnp.float32,
+    ).astype(jnp.bfloat16)
+    adapter_copies = []
+    for step in range(1, tp_size):
+        device = {"ctx": ctx, "tp": lax.rem(tp + step, tp_size)}
+        adapter_copies.append(
+            push(
+                adapter_parts.at[0],
+                adapter_parts.at[step],
+                send_ad.at[step],
+                recv_ad.at[step],
+                device,
+            )
+        )
+    for copy in adapter_copies:
+        copy.wait()
+    adapter_total = adapter_parts[0].astype(jnp.float32)
+    for step in range(1, tp_size):
+        adapter_total += adapter_parts[step].astype(jnp.float32)
+    adapter_sum[...] = adapter_total.astype(jnp.bfloat16)
+    adapter_out[:, token_rows(ctx)] = adapter_sum[...]
+    later = []
+    for step in range(1, ctx_size):
+        device = {"ctx": lax.rem(ctx + step, ctx_size), "tp": tp}
+        later.append(
+            push(
+                adapter_sum,
+                adapter_out.at[:, token_rows(ctx)],
+                send_adsum.at[step],
+                recv_adsum.at[step],
+                device,
+            )
+        )
+
+    def exchange(kind, src, dst, step):
+        other = lax.rem(ctx + step, ctx_size)
+        return describe(
+            src.at[pl.ds(pl.multiple_of(other * ch_rows, 16), ch_rows), :],
+            dst.at[:, token_rows(ctx)],
+            send_row.at[kind, step],
+            recv_row.at[kind, step],
+            {"ctx": other, "tp": tp},
+        )
+
+    pairs = ((filter_ref, filter_out), (gated_ref, gated_out), (outer_ref, outer_out))
+    my_rows = pl.ds(pl.multiple_of(ctx * ch_rows, 16), ch_rows)
+    for src, dst in pairs:
+        dst[:, token_rows(ctx)] = src[my_rows, :]
+
+    def part_copy(block, step):
+        other = lax.rem(tp + step, tp_size)
+        return describe(
+            partial.at[block, step],
+            landed.at[block, step],
+            send_part.at[block, step],
+            recv_part.at[block, step],
+            {"ctx": ctx, "tp": other},
+        )
+
+    place = ctx * tp_size + tp
+    goal_ctx, goal_tp = lax.rem(place, ctx_size), place // ctx_size
+    stays = jnp.logical_and(goal_ctx == ctx, goal_tp == tp)
+
+    def sum_copy(block):
+        return describe(
+            summed.at[block],
+            back_out.at[:, token_rows(block)],
+            send_sum.at[block],
+            recv_sum.at[block],
+            {"ctx": goal_ctx, "tp": goal_tp},
+        )
+
+    def multiply(block):
+        for step in list(range(1, tp_size)) + [0]:
+            other = lax.rem(tp + step, tp_size)
+            partial[block, step] = lax.dot_general(
+                weight_ref[pl.ds(pl.multiple_of(other * rows, 16), rows), :],
+                whole_out[token_rows(block), :],
+                (((1,), (1,)), ((), ())),
+                preferred_element_type=jnp.float32,
+            ).astype(jnp.bfloat16)
+            if step:
+                part_copy(block, step).start()
+
+    def finish(i):
+        hop, way, block, valid = stage(i)
+
+        @pl.when(valid)
+        def _():
+            total = partial[block, 0].astype(jnp.float32)
+            for step in range(1, tp_size):
+                part_copy(block, step).wait_recv()
+                total += landed[block, step].astype(jnp.float32)
+            summed[block] = total.astype(jnp.bfloat16)
+
+            @pl.when(stays)
+            def _():
+                back_out[:, token_rows(block)] = summed[block]
+
+            @pl.when(jnp.logical_not(stays))
+            def _():
+                sum_copy(block).start()
+
+    def body(i, carry):
+        hop, way, block, valid = stage(i)
+
+        @pl.when(valid)
+        def _():
+            @pl.when(i > 0)
+            def _():
+                relay(way, hop - 1, block).wait_recv()
+
+                @pl.when(can_relay(way))
+                def _():
+                    relay(way, hop, block).start()
+
+            multiply(block)
+
+        @pl.when(i == exchange_step)
+        def _():
+            for kind, (src, dst) in enumerate(pairs):
+                for step in range(1, ctx_size):
+                    exchange(kind, src, dst, step).start()
+
+        pl.when(i > 0)(lambda: finish(i - 1))
+        return carry
+
+    lax.fori_loop(0, steps, body, 0)
+    finish(steps - 1)
+
+    for way in range(2):
+        for hop in range(ctx_size - 1):
+            block = ctx - hop if way == 0 else ctx + hop
+            held = jnp.logical_and(block >= 0, block < ctx_size)
+            pl.when(jnp.logical_and(held, can_relay(way)))(
+                lambda way=way, hop=hop, block=block: relay(way, hop, block).wait_send()
+            )
+    for block in range(ctx_size):
+        for step in range(1, tp_size):
+            part_copy(block, step).wait_send()
+    for copy in later:
+        copy.wait()
+    for kind, (src, dst) in enumerate(pairs):
+        for step in range(1, ctx_size):
+            exchange(kind, src, dst, step).wait()
+
+    @pl.when(jnp.logical_not(stays))
+    def _():
+        for block in range(ctx_size):
+            sum_copy(block).wait()
+
+
+def project_all(cotangent, weight, up_factor, masked_filter, gated, outer_gate):
+    ctx_size, tp_size = lax.axis_size("ctx"), lax.axis_size("tp")
+    width, features = cotangent.shape
+    length = width * ctx_size
+    rows = weight.shape[0] // tp_size
+    rank = up_factor.shape[0]
+    channels = jax.ShapeDtypeStruct((gated.shape[0] // ctx_size, length), jnp.bfloat16)
+    dma = pltpu.SemaphoreType.DMA
+    return pl.pallas_call(
+        functools.partial(project_kernel, ctx_size, tp_size),
+        out_shape=(
+            jax.ShapeDtypeStruct((length, features), jnp.bfloat16),
+            channels,
+            channels,
+            channels,
+            jax.ShapeDtypeStruct((rows, length), jnp.bfloat16),
+            jax.ShapeDtypeStruct((rank, length), jnp.bfloat16),
+        ),
+        in_specs=[pl.BlockSpec(memory_space=pltpu.VMEM)] * 6,
+        out_specs=(pl.BlockSpec(memory_space=pltpu.VMEM),) * 6,
+        scratch_shapes=[
+            pltpu.VMEM((ctx_size, tp_size, rows, width), jnp.bfloat16),
+            pltpu.VMEM((ctx_size, tp_size, rows, width), jnp.bfloat16),
+            pltpu.VMEM((ctx_size, rows, width), jnp.bfloat16),
+            pltpu.VMEM((tp_size, rank, width), jnp.bfloat16),
+            pltpu.VMEM((rank, width), jnp.bfloat16),
+            dma((2, ctx_size)),
+            dma((2, ctx_size)),
+            dma((ctx_size, tp_size)),
+            dma((ctx_size, tp_size)),
+            dma((ctx_size,)),
+            dma((ctx_size,)),
+            dma((3, ctx_size)),
+            dma((3, ctx_size)),
+            dma((tp_size,)),
+            dma((tp_size,)),
+            dma((ctx_size,)),
+            dma((ctx_size,)),
+        ],
+        compiler_params=pltpu.CompilerParams(
+            collective_id=2, has_side_effects=True, vmem_limit_bytes=48 << 20
+        ),
+    )(cotangent, weight, up_factor, masked_filter, gated, outer_gate)
+
+
 def token_by_kernel(count, shape, rank):
     return count <= kernel_peers and shape[1] <= dense_length and rank * shape[1] == count * 2048
 
@@ -330,36 +613,53 @@
         jnp.zeros_like(channel_filter_lags),
     ).astype(jnp.bfloat16)
     gated = product_bf(inner_gate_proj, value_projection)
-    whole_cotangent = lax.all_gather(output_cotangent, "ctx", axis=0, tiled=True)
-    filter_ch, gated_ch, outer_ch = lax.all_to_all(
-        jnp.stack([masked_filter, gated, outer_gate_proj]),
-        "ctx",
-        split_axis=1,
-        concat_axis=2,
-        tiled=True,
-    )
+    by_kernel = token_by_kernel(
+        ctx_size * tp_size,
+        (gated.shape[0] // ctx_size, tok_rows * ctx_size),
+        adapter_down_factor.shape[1],
+    )
+    if by_kernel:
+        whole_cotangent, filter_ch, gated_ch, outer_ch, output_backward, adapter_t = project_all(
+            output_cotangent,
+            output_weight,
+            adapter_up_factor,
+            masked_filter,
+            gated,
+            outer_gate_proj,
+        )
+        output_backward = output_backward.astype(jnp.float32)
+        adapter_backward = adapter_t.T
+    else:
+        whole_cotangent = lax.all_gather(output_cotangent, "ctx", axis=0, tiled=True)
+        filter_ch, gated_ch, outer_ch = lax.all_to_all(
+            jnp.stack([masked_filter, gated, outer_gate_proj]),
+            "ctx",
+            split_axis=1,
+            concat_axis=2,
+            tiled=True,
+        )
+        partial = lax.dot_general(
+            output_weight,
+            whole_cotangent,
+            (((1,), (1,)), ((), ())),
+            preferred_element_type=jnp.float32,
+        ).astype(jnp.bfloat16)
+        adapter_backward = lax.psum(
+            lax.dot_general(
+                whole_cotangent,
+                adapter_up_factor,
+                (((1,), (1,)), ((), ())),
+                preferred_element_type=jnp.float32,
+            ).astype(jnp.bfloat16),
+            "tp",
+        )
+        scattered = lax.psum_scatter(partial, "tp", scatter_dimension=0, tiled=True)
+        moves = [(i, (i % ctx_size) * tp_size + i // ctx_size) for i in range(ctx_size * tp_size)]
+        output_backward = lax.ppermute(scattered, ("ctx", "tp"), moves).astype(jnp.float32)
     rows = filter_ch.shape[0]
     down_rows = lax.dynamic_slice_in_dim(
         adapter_down_factor, lax.axis_index("ctx") * rows, rows, axis=0
     )
-    partial = lax.dot_general(
-        output_weight,
-        whole_cotangent,
-        (((1,), (1,)), ((), ())),
-        preferred_element_type=jnp.float32,
-    ).astype(jnp.bfloat16)
-    adapter_backward = lax.psum(
-        lax.dot_general(
-            whole_cotangent,
-            adapter_up_factor,
-            (((1,), (1,)), ((), ())),
-            preferred_element_type=jnp.float32,
-        ).astype(jnp.bfloat16),
-        "tp",
-    )
-    scattered = lax.psum_scatter(partial, "tp", scatter_dimension=0, tiled=True)
-    moves = [(i, (i % ctx_size) * tp_size + i // ctx_size) for i in range(ctx_size * tp_size)]
-    output_backward = lax.ppermute(scattered, ("ctx", "tp"), moves).astype(jnp.float32)
     adapter_term = lax.dot_general(
         down_rows,
         adapter_backward,
@@ -374,7 +674,7 @@
         conv_ch, grad_gated_ch = convolve(filter_ch.astype(jnp.float32), gated_ch, grad_conv)
     block_output = product_bf(outer_ch, conv_ch)
     outer_grad_ch = product_bf(projected_gradient, conv_ch)
-    if token_by_kernel(ctx_size * tp_size, filter_ch.shape, adapter_down_factor.shape[1]):
+    if by_kernel:
         token_t = lax.dot_general(
             down_rows,
             block_output,

time: 262 us -> 186 us (0.71)
  waiting for transfers between devices: 159 us -> 0 us
  Pallas kernels: 33.8 us -> 169 us
  matrix products: 30.9 us -> 7.96 us
  between operations: 14 us -> 0.84 us
  starting transfers between devices: 9.27 us -> 0 us
  local copies, waits for them, and re-layouts: 11.1 us -> 3.39 us
    pallas_call x0 -> x1, Pallas kernels: none -> 130 us  [project_all(): pl.pallas_call(functools.partial(project_kernel, ctx_size, tp_size), out_...]
    all_gather x1 -> x0, waiting for transfers between devices: 85.1 us -> none  [local(): lax.all_gather(output_cotangent, 'ctx', axis=0, tiled=True)]
    all_to_all x1 -> x0, waiting for transfers between devices: 48.4 us -> none  [local(): lax.all_to_all(jnp.stack([masked_filter, gated, outer_gate_proj]), 'ctx',...]
    psum x1 -> x0, waiting for transfers between devices: 24.5 us -> none  [local(): lax.psum(lax.dot_general(whole_cotangent, adapter_up_factor, (((1,), (1,)...]
    dot_general x2 -> x0, matrix products: 13.5 us -> none  [the longest x1 9.39 us: local(): lax.dot_general(output_weight, whole_cotangent, (((1,), (1,)), ((), ())),...]
    ppermute x1 -> x0, starting transfers between devices: 5.48 us -> none  [local(): lax.ppermute(scattered, ('ctx', 'tp'), moves).astype(jnp.float32)]
    pallas_call x1, Pallas kernels: 33.8 us -> 39.1 us  [return_all(): pl.pallas_call(functools.partial(return_kernel, ctx_size, tp_size), out_s...]
    dot_general x3, matrix products: 8.89 us -> 3.74 us  [dense_spectrum(): spec = jnp.dot(field, table, preferred_element_type=jnp.float32)]
  transfers between devices with their start and end apart: 5 -> 0, of which waited for: 3 -> 0; matrix products, arithmetic and copies ran while one was open for 8% -> 0% of each run, Pallas kernels for 0% -> 0%
where the time goes in v3:
time: 186 us
  Pallas kernels  169 us (91%)
  matrix products  7.96 us (4%)
  other arithmetic  4.77 us (3%)
  local copies, waits for them, and re-layouts  3.39 us (2%)
    pallas_call x1, Pallas kernels, project_all(): pl.pallas_call(functools.partial(project_kernel, ctx_size, tp_size), out_...  130 us
    pallas_call x1, Pallas kernels, return_all(): pl.pallas_call(functools.partial(return_kernel, ctx_size, tp_size), out_s...  39.1 us
    dot_general x3, matrix products, dense_spectrum(): spec = jnp.dot(field, table, preferred_element_type=jnp.float32)  3.74 us

profile of v3, /device:TPU:0, one launch (start us, length us, event | category | flops | bytes accessed | tf_op | source)
XLA Modules:
  0.0 186.0 jit_solution(7430569453870647935)
XLA Ops:
  0.6 0.0 copy-start
  0.6 0.0 copy-start.4
  0.7 0.0 copy-start.2
  0.7 0.0 copy-start.3
  0.7 1.6 select_convert_fusion.filter_ref
  2.3 1.3 fusion.5.gated_ref
  3.6 0.0 copy-done.4
  3.6 0.0 copy-done.2
  3.6 0.0 copy-done.3
  3.6 0.0 copy-start.7
  3.6 129.9 %shard_map.137 = (bf16[1024,2048]{1,0:T(8,128)(2,1)}, bf16[256,1024]{1,0:T(8,128)(2,1)S(1)}, bf16[256,1024]{1,0:T(8,128)(2,1)S(1)}, bf16[256,1024]{1,0:T(8,128)(...) custom-call(bf16[256,2048]{1,0:T(8,128)(2,1)S(1)} %copy-done.2, bf16[1024,2048]{1,0:T(8,128)(2,1)} %weight_ref.1, ...), custom_call_target="tpu_custom_call" | custom-call | tf_op jit(solution)/shard_map/pallas_call | solution.py:553
  133.5 0.0 copy-done
  133.5 0.3 fusion.4
  133.9 0.0 copy-done.7
  133.9 1.2 fusion.21
  135.1 0.0 copy-start.5
  135.2 1.2 fusion.11
  136.4 0.3 copy-done.5
  136.7 0.0 copy-start.6
  136.7 0.8 fusion.13
  137.5 0.8 copy-done.6
  138.3 0.8 fusion.2.grad_ref
  139.1 1.2 fusion.22
  140.4 0.9 fusion.14
  141.3 0.0 copy-start.1
  141.3 0.9 fusion.7
  142.2 0.3 convolution_convert_fusion.1.down_ref
  142.5 0.2 convolution_convert_fusion.token_ref
  142.7 0.7 copy-done.1
  143.5 0.0 copy-start.8
  143.5 0.0 copy-start.9
  143.5 39.1 %shard_map.138 = (bf16[1024,256]{1,0:T(8,128)(2,1)S(1)}, bf16[1024,256]{1,0:T(8,128)(2,1)S(1)}, bf16[32,1024]{1,0:T(8,128)(2,1)S(1)}, f32[32,2048]{1,0:T(8,128)S(1)}) custom-call(bf16[256,1024]{1,0:T(8,128)(2,1)S(1)} %fusion.2.grad_ref, bf16[256,1024]{1,0:T(8,128)(2,1)S(1)} %get-tuple-element.27.outer_ref, ...), custom_call_target="tpu_custom_call" | custom-call | tf_op jit(solution)/shard_map/pallas_call | solution.py:280
  182.6 0.7 multiply_bitcast_fusion
  183.3 0.0 copy-done.8
  183.3 0.0 copy-done.9
  183.3 1.2 fusion.10
  184.5 0.8 copy.17
  185.3 0.7 copy.18
  (1 shorter events, 0.0 us)
Async XLA Ops:
  0.6 132.9 %copy-start = (bf16[1024,32]{0,1:T(8,128)(2,1)S(1)}, bf16[1024,32]{0,1:T(8,128)(2,1)}, u32[]{:S(2)}) copy-start(bf16[1024,32]{0,1:T(8,128)(2,1)} %param.17) | copy-start | bytes 196612
  0.6 2.9 %copy-start.4 = (bf16[32,2048]{1,0:T(8,128)(2,1)S(1)}, bf16[32,2048]{1,0:T(8,128)(2,1)}, u32[]{:S(2)}) copy-start(bf16[32,2048]{1,0:T(8,128)(2,1)} %up_ref.1) | copy-start | bytes 393220
  0.7 2.9 %copy-start.2 = (bf16[256,2048]{1,0:T(8,128)(2,1)S(1)}, bf16[256,2048]{1,0:T(8,128)(2,1)}, u32[]{:S(2)}) copy-start(bf16[256,2048]{1,0:T(8,128)(2,1)} %cotangent_ref.1) | copy-start | bytes 3145732
  0.7 2.9 %copy-start.3 = (bf16[1024,256]{1,0:T(8,128)(2,1)S(1)}, bf16[1024,256]{1,0:T(8,128)(2,1)}, u32[]{:S(2)}) copy-start(bf16[1024,256]{1,0:T(8,128)(2,1)} %outer_ref.1) | copy-start | bytes 1572868
  3.6 130.3 %copy-start.7 = (bf16[1024,2048]{1,0:T(8,128)(2,1)S(1)}, bf16[1024,2048]{1,0:T(8,128)(2,1)}, u32[]{:S(2)}) copy-start(bf16[1024,2048]{1,0:T(8,128)(2,1)} %constant.19.clone) | copy-start | bytes 12582916
  135.1 1.6 copy-start.5
  136.7 1.6 copy-start.6
  141.3 2.2 %copy-start.1 = (bf16[1024,2048]{1,0:T(8,128)(2,1)S(1)}, bf16[1024,2048]{1,0:T(8,128)(2,1)}, u32[]{:S(2)}) copy-start(bf16[1024,2048]{1,0:T(8,128)(2,1)} %get-tuple-element.20.cotangent_ref) | copy-start | bytes 12582916
  143.5 39.8 %copy-start.8 = (bf16[1024,256]{1,0:T(8,128)(2,1)S(1)}, bf16[1024,256]{1,0:T(8,128)(2,1)}, u32[]{:S(2)}) copy-start(bf16[1024,256]{1,0:T(8,128)(2,1)} %param.10) | copy-start | bytes 1572868
  143.5 39.8 %copy-start.9 = (bf16[1024,256]{1,0:T(8,128)(2,1)S(1)}, bf16[1024,256]{1,0:T(8,128)(2,1)}, u32[]{:S(2)}) copy-start(bf16[1024,256]{1,0:T(8,128)(2,1)} %param.12) | copy-start | bytes 1572868

commit v4 on v3

--- a/solution.py
+++ b/solution.py
@@ -304,7 +304,7 @@
     )(grad_gated_ch, outer_grad_ch, token_t, down_t, whole_cotangent)
 
 
-exchange_step = 3
+exchange_step = 4
 
 
 def project_kernel(
@@ -367,14 +367,15 @@
         block = ctx + hop - 2 * odd * hop
         return hop, 1 - odd, block, jnp.logical_and(block >= 0, block < ctx_size)
 
-    def relay(way, hop, block):
+    def relay(way, hop, block, half):
         target = lax.rem(ctx + ctx_size + 1 - 2 * way, ctx_size)
-        held = whole_out.at[token_rows(block), :]
+        top = pl.multiple_of(block * width + half * (width // 2), 16)
+        held = whole_out.at[pl.ds(top, width // 2), :]
         return describe(
             held,
             held,
-            send_relay.at[way, hop],
-            recv_relay.at[way, hop + 1],
+            send_relay.at[2 * way + half, hop],
+            recv_relay.at[2 * way + half, hop + 1],
             {"ctx": target, "tp": tp},
         )
 
@@ -383,8 +384,9 @@
         return jnp.logical_and(target >= 0, target < ctx_size)
 
     whole_out[token_rows(ctx), :] = cotangent_ref[...]
-    for way in range(2):
-        pl.when(can_relay(way))(lambda way=way: relay(way, 0, ctx).start())
+    for half in range(2):
+        for way in range(2):
+            pl.when(can_relay(way))(lambda way=way, half=half: relay(way, 0, ctx, half).start())
 
     adapter_parts[0] = lax.dot_general(
         up_ref[...],
@@ -493,20 +495,27 @@
             def _():
                 sum_copy(block).start()
 
+    def pass_on(side, hop, half):
+        block = ctx - hop if side == 0 else ctx + hop
+
+        @pl.when(jnp.logical_and(block >= 0, block < ctx_size))
+        def _():
+            relay(side, hop - 1, block, half).wait_recv()
+
+            @pl.when(can_relay(side))
+            def _():
+                relay(side, hop, block, half).start()
+
     def body(i, carry):
         hop, way, block, valid = stage(i)
 
-        @pl.when(valid)
+        @pl.when(way == 0)
         def _():
-            @pl.when(i > 0)
-            def _():
-                relay(way, hop - 1, block).wait_recv()
-
-                @pl.when(can_relay(way))
-                def _():
-                    relay(way, hop, block).start()
-
-            multiply(block)
+            for half in range(2):
+                for side in range(2):
+                    pass_on(side, hop, half)
+
+        pl.when(valid)(lambda: multiply(block))
 
         @pl.when(i == exchange_step)
         def _():
@@ -524,9 +533,12 @@
         for hop in range(ctx_size - 1):
             block = ctx - hop if way == 0 else ctx + hop
             held = jnp.logical_and(block >= 0, block < ctx_size)
-            pl.when(jnp.logical_and(held, can_relay(way)))(
-                lambda way=way, hop=hop, block=block: relay(way, hop, block).wait_send()
-            )
+            for half in range(2):
+                pl.when(jnp.logical_and(held, can_relay(way)))(
+                    lambda way=way, hop=hop, block=block, half=half: relay(
+                        way, hop, block, half
+                    ).wait_send()
+                )
     for block in range(ctx_size):
         for step in range(1, tp_size):
             part_copy(block, step).wait_send()
@@ -568,8 +580,8 @@
             pltpu.VMEM((ctx_size, rows, width), jnp.bfloat16),
             pltpu.VMEM((tp_size, rank, width), jnp.bfloat16),
             pltpu.VMEM((rank, width), jnp.bfloat16),
-            dma((2, ctx_size)),
-            dma((2, ctx_size)),
+            dma((4, ctx_size)),
+            dma((4, ctx_size)),
             dma((ctx_size, tp_size)),
             dma((ctx_size, tp_size)),
             dma((ctx_size,)),

time: 186 us -> 176 us (0.946)
  Pallas kernels: 169 us -> 159 us
    pallas_call x1, Pallas kernels: 130 us -> 122 us  [project_all(): pl.pallas_call(functools.partial(project_kernel, ctx_size, tp_size), out_...]
    pallas_call x1, Pallas kernels: 39.1 us -> 37.1 us  [return_all(): pl.pallas_call(functools.partial(return_kernel, ctx_size, tp_size), out_s...]
where the time goes in v4:
time: 176 us
  Pallas kernels  159 us (90%)
  matrix products  7.96 us (5%)
  other arithmetic  4.77 us (3%)
  local copies, waits for them, and re-layouts  3.39 us (2%)
    pallas_call x1, Pallas kernels, project_all(): pl.pallas_call(functools.partial(project_kernel, ctx_size, tp_size), out_...  122 us
    pallas_call x1, Pallas kernels, return_all(): pl.pallas_call(functools.partial(return_kernel, ctx_size, tp_size), out_s...  37.1 us
    dot_general x3, matrix products, dense_spectrum(): spec = jnp.dot(field, table, preferred_element_type=jnp.float32)  3.74 us

profile of v4, /device:TPU:0, one launch (start us, length us, event | category | flops | bytes accessed | tf_op | source)
XLA Modules:
  0.0 176.0 jit_solution(13768459495456723794)
XLA Ops:
  0.6 0.0 copy-start
  0.6 0.0 copy-start.4
  0.7 0.0 copy-start.2
  0.7 0.0 copy-start.3
  0.7 1.6 select_convert_fusion.filter_ref
  2.3 1.3 fusion.5.gated_ref
  3.6 0.0 copy-done.4
  3.6 0.0 copy-done.2
  3.6 0.0 copy-done.3
  3.6 0.0 copy-start.7
  3.6 121.9 %shard_map.137 = (bf16[1024,2048]{1,0:T(8,128)(2,1)}, bf16[256,1024]{1,0:T(8,128)(2,1)S(1)}, bf16[256,1024]{1,0:T(8,128)(2,1)S(1)}, bf16[256,1024]{1,0:T(8,128)(...) custom-call(bf16[256,2048]{1,0:T(8,128)(2,1)S(1)} %copy-done.2, bf16[1024,2048]{1,0:T(8,128)(2,1)} %weight_ref.1, ...), custom_call_target="tpu_custom_call" | custom-call | tf_op jit(solution)/shard_map/pallas_call | solution.py:565
  125.5 0.0 copy-done
  125.6 0.3 fusion.4
  125.9 0.0 copy-done.7
  125.9 1.2 fusion.21
  127.1 0.0 copy-start.5
  127.2 1.2 fusion.11
  128.4 0.3 copy-done.5
  128.7 0.0 copy-start.6
  128.7 0.8 fusion.13
  129.5 0.8 copy-done.6
  130.3 0.8 fusion.2.grad_ref
  131.1 1.2 fusion.22
  132.4 0.9 fusion.14
  133.3 0.0 copy-start.1
  133.3 0.9 fusion.7
  134.2 0.3 convolution_convert_fusion.1.down_ref
  134.5 0.2 convolution_convert_fusion.token_ref
  134.7 0.7 copy-done.1
  135.5 0.0 copy-start.8
  135.5 0.0 copy-start.9
  135.5 37.1 %shard_map.138 = (bf16[1024,256]{1,0:T(8,128)(2,1)S(1)}, bf16[1024,256]{1,0:T(8,128)(2,1)S(1)}, bf16[32,1024]{1,0:T(8,128)(2,1)S(1)}, f32[32,2048]{1,0:T(8,128)S(1)}) custom-call(bf16[256,1024]{1,0:T(8,128)(2,1)S(1)} %fusion.2.grad_ref, bf16[256,1024]{1,0:T(8,128)(2,1)S(1)} %get-tuple-element.27.outer_ref, ...), custom_call_target="tpu_custom_call" | custom-call | tf_op jit(solution)/shard_map/pallas_call | solution.py:280
  172.6 0.7 multiply_bitcast_fusion
  173.3 0.0 copy-done.8
  173.3 0.0 copy-done.9
  173.3 1.2 fusion.10
  174.5 0.8 copy.17
  175.3 0.7 copy.18
  (1 shorter events, 0.0 us)
Async XLA Ops:
  0.6 124.9 %copy-start = (bf16[1024,32]{0,1:T(8,128)(2,1)S(1)}, bf16[1024,32]{0,1:T(8,128)(2,1)}, u32[]{:S(2)}) copy-start(bf16[1024,32]{0,1:T(8,128)(2,1)} %param.17) | copy-start | bytes 196612
  0.6 2.9 %copy-start.4 = (bf16[32,2048]{1,0:T(8,128)(2,1)S(1)}, bf16[32,2048]{1,0:T(8,128)(2,1)}, u32[]{:S(2)}) copy-start(bf16[32,2048]{1,0:T(8,128)(2,1)} %up_ref.1) | copy-start | bytes 393220
  0.7 2.9 %copy-start.2 = (bf16[256,2048]{1,0:T(8,128)(2,1)S(1)}, bf16[256,2048]{1,0:T(8,128)(2,1)}, u32[]{:S(2)}) copy-start(bf16[256,2048]{1,0:T(8,128)(2,1)} %cotangent_ref.1) | copy-start | bytes 3145732
  0.7 2.9 %copy-start.3 = (bf16[1024,256]{1,0:T(8,128)(2,1)S(1)}, bf16[1024,256]{1,0:T(8,128)(2,1)}, u32[]{:S(2)}) copy-start(bf16[1024,256]{1,0:T(8,128)(2,1)} %outer_ref.1) | copy-start | bytes 1572868
  3.6 122.3 %copy-start.7 = (bf16[1024,2048]{1,0:T(8,128)(2,1)S(1)}, bf16[1024,2048]{1,0:T(8,128)(2,1)}, u32[]{:S(2)}) copy-start(bf16[1024,2048]{1,0:T(8,128)(2,1)} %constant.19.clone) | copy-start | bytes 12582916
  127.1 1.6 copy-start.5
  128.7 1.6 copy-start.6
  133.3 2.2 %copy-start.1 = (bf16[1024,2048]{1,0:T(8,128)(2,1)S(1)}, bf16[1024,2048]{1,0:T(8,128)(2,1)}, u32[]{:S(2)}) copy-start(bf16[1024,2048]{1,0:T(8,128)(2,1)} %get-tuple-element.20.cotangent_ref) | copy-start | bytes 12582916
  135.5 37.8 %copy-start.8 = (bf16[1024,256]{1,0:T(8,128)(2,1)S(1)}, bf16[1024,256]{1,0:T(8,128)(2,1)}, u32[]{:S(2)}) copy-start(bf16[1024,256]{1,0:T(8,128)(2,1)} %param.10) | copy-start | bytes 1572868
  135.5 37.8 %copy-start.9 = (bf16[1024,256]{1,0:T(8,128)(2,1)S(1)}, bf16[1024,256]{1,0:T(8,128)(2,1)}, u32[]{:S(2)}) copy-start(bf16[1024,256]{1,0:T(8,128)(2,1)} %param.12) | copy-start | bytes 1572868

commit v5 on v4

--- a/solution.py
+++ b/solution.py
@@ -180,7 +180,7 @@
     outer_ref,
     token_ref,
     down_ref,
-    cotangent_ref,
+    cotangent_any,
     grad_out,
     outer_out,
     down_out,
@@ -194,7 +194,11 @@
     send_row,
     recv_row,
     local_sem,
+    cotangent_ref,
+    load_sem,
 ):
+    load = pltpu.make_async_copy(cotangent_any, cotangent_ref, load_sem)
+    load.start()
     me, count, peer = position()
     ctx, tp = lax.axis_index("ctx"), lax.axis_index("tp")
     rows, length = grad_ref.shape
@@ -263,6 +267,7 @@
     own.wait()
     for copy in copies:
         copy.wait()
+    load.wait()
     up_out[...] = adapter_scale * jnp.dot(
         whole[...], cotangent_ref[...], preferred_element_type=jnp.float32
     )
@@ -285,7 +290,8 @@
             jax.ShapeDtypeStruct((rank, rows * ctx_size), jnp.bfloat16),
             jax.ShapeDtypeStruct((rank, whole_cotangent.shape[1]), jnp.float32),
         ),
-        in_specs=[pl.BlockSpec(memory_space=pltpu.VMEM)] * 5,
+        in_specs=[pl.BlockSpec(memory_space=pltpu.VMEM)] * 4
+        + [pl.BlockSpec(memory_space=pl.ANY)],
         out_specs=(pl.BlockSpec(memory_space=pltpu.VMEM),) * 4,
         scratch_shapes=[
             pltpu.VMEM((count, 16, 128), jnp.bfloat16),
@@ -297,6 +303,8 @@
             dma((3, ctx_size)),
             dma((3, ctx_size)),
             dma,
+            pltpu.VMEM(whole_cotangent.shape, jnp.bfloat16),
+            dma,
         ],
         compiler_params=pltpu.CompilerParams(
             collective_id=1, has_side_effects=True, vmem_limit_bytes=40 << 20
@@ -311,12 +319,12 @@
     ctx_size,
     tp_size,
     cotangent_ref,
-    weight_ref,
+    weight_any,
     up_ref,
     filter_ref,
     gated_ref,
     outer_ref,
-    whole_out,
+    whole_any,
     filter_out,
     gated_out,
     outer_out,
@@ -339,7 +347,13 @@
     recv_ad,
     send_adsum,
     recv_adsum,
+    weight_ref,
+    whole_out,
+    load_sem,
+    store_sem,
 ):
+    load = pltpu.make_async_copy(weight_any, weight_ref, load_sem)
+    load.start()
     me, count, peer = position()
     ctx, tp = lax.axis_index("ctx"), lax.axis_index("tp")
     width = cotangent_ref.shape[0]
@@ -526,7 +540,10 @@
         pl.when(i > 0)(lambda: finish(i - 1))
         return carry
 
+    load.wait()
     lax.fori_loop(0, steps, body, 0)
+    store = pltpu.make_async_copy(whole_out, whole_any, store_sem)
+    store.start()
     finish(steps - 1)
 
     for way in range(2):
@@ -553,6 +570,8 @@
         for block in range(ctx_size):
             sum_copy(block).wait()
 
+    store.wait()
+
 
 def project_all(cotangent, weight, up_factor, masked_filter, gated, outer_gate):
     ctx_size, tp_size = lax.axis_size("ctx"), lax.axis_size("tp")
@@ -572,8 +591,12 @@
             jax.ShapeDtypeStruct((rows, length), jnp.bfloat16),
             jax.ShapeDtypeStruct((rank, length), jnp.bfloat16),
         ),
-        in_specs=[pl.BlockSpec(memory_space=pltpu.VMEM)] * 6,
-        out_specs=(pl.BlockSpec(memory_space=pltpu.VMEM),) * 6,
+        in_specs=[
+            pl.BlockSpec(memory_space=pl.ANY if arg == 1 else pltpu.VMEM) for arg in range(6)
+        ],
+        out_specs=tuple(
+            pl.BlockSpec(memory_space=pl.ANY if out == 0 else pltpu.VMEM) for out in range(6)
+        ),
         scratch_shapes=[
             pltpu.VMEM((ctx_size, tp_size, rows, width), jnp.bfloat16),
             pltpu.VMEM((ctx_size, tp_size, rows, width), jnp.bfloat16),
@@ -592,6 +615,10 @@
             dma((tp_size,)),
             dma((ctx_size,)),
             dma((ctx_size,)),
+            pltpu.VMEM(weight.shape, jnp.bfloat16),
+            pltpu.VMEM((length, features), jnp.bfloat16),
+            dma,
+            dma,
         ],
         compiler_params=pltpu.CompilerParams(
             collective_id=2, has_side_effects=True, vmem_limit_bytes=48 << 20

time: 176 us -> 172 us (0.977)
  Pallas kernels: 159 us -> 155 us
    pallas_call x1, Pallas kernels: 122 us -> 118 us  [project_all(): pl.pallas_call(functools.partial(project_kernel, ctx_size, tp_size), out_...]
where the time goes in v5:
time: 172 us
  Pallas kernels  155 us (90%)
  matrix products  7.96 us (5%)
  other arithmetic  4.77 us (3%)
  local copies, waits for them, and re-layouts  3.39 us (2%)
    pallas_call x1, Pallas kernels, project_all(): pl.pallas_call(functools.partial(project_kernel, ctx_size, tp_size), out_...  118 us
    pallas_call x1, Pallas kernels, return_all(): pl.pallas_call(functools.partial(return_kernel, ctx_size, tp_size), out_s...  37.5 us
    dot_general x3, matrix products, dense_spectrum(): spec = jnp.dot(field, table, preferred_element_type=jnp.float32)  3.74 us

profile of v5, /device:TPU:0, one launch (start us, length us, event | category | flops | bytes accessed | tf_op | source)
XLA Modules:
  0.0 172.1 jit_solution(7876003819570825442)
XLA Ops:
  0.6 0.0 copy-start
  0.6 0.0 copy-start.4
  0.7 0.0 copy-start.2
  0.7 0.0 copy-start.3
  0.7 1.6 select_convert_fusion.filter_ref
  2.3 1.3 fusion.5.gated_ref
  3.6 0.0 copy-done.4
  3.6 0.0 copy-done.2
  3.6 0.0 copy-done.3
  3.6 0.0 copy-start.7
  3.6 117.6 %shard_map.137 = (bf16[1024,2048]{1,0:T(8,128)(2,1)}, bf16[256,1024]{1,0:T(8,128)(2,1)S(1)}, bf16[256,1024]{1,0:T(8,128)(2,1)S(1)}, bf16[256,1024]{1,0:T(8,128)(...) custom-call(bf16[256,2048]{1,0:T(8,128)(2,1)S(1)} %copy-done.2, bf16[1024,2048]{1,0:T(8,128)(2,1)} %weight_any.1, ...), custom_call_target="tpu_custom_call" | custom-call | tf_op jit(solution)/shard_map/pallas_call | solution.py:584
  121.3 0.0 copy-done
  121.3 0.3 fusion.4
  121.6 0.0 copy-done.7
  121.6 1.2 fusion.21
  122.9 0.0 copy-start.5
  122.9 1.2 fusion.11
  124.2 0.3 copy-done.5
  124.5 0.0 copy-start.6
  124.5 0.8 fusion.13
  125.3 0.8 copy-done.6
  126.1 0.8 fusion.2.grad_ref
  126.9 1.2 fusion.22
  128.1 0.9 fusion.14
  129.0 0.0 copy-start.1
  129.0 0.9 fusion.7
  130.0 0.3 convolution_convert_fusion.1.down_ref
  130.2 0.2 convolution_convert_fusion.token_ref
  130.5 0.7 copy-done.1
  131.2 0.0 copy-start.8
  131.2 0.0 copy-start.9
  131.2 37.5 %shard_map.138 = (bf16[1024,256]{1,0:T(8,128)(2,1)S(1)}, bf16[1024,256]{1,0:T(8,128)(2,1)S(1)}, bf16[32,1024]{1,0:T(8,128)(2,1)S(1)}, f32[32,2048]{1,0:T(8,128)S(1)}) custom-call(bf16[256,1024]{1,0:T(8,128)(2,1)S(1)} %fusion.2.grad_ref, bf16[256,1024]{1,0:T(8,128)(2,1)S(1)} %get-tuple-element.27.outer_ref, ...), custom_call_target="tpu_custom_call" | custom-call | tf_op jit(solution)/shard_map/pallas_call | solution.py:285
  168.7 0.7 multiply_bitcast_fusion
  169.3 0.0 copy-done.8
  169.3 0.0 copy-done.9
  169.3 1.2 fusion.10
  170.6 0.8 copy.17
  171.3 0.7 copy.18
  (1 shorter events, 0.0 us)
Async XLA Ops:
  0.6 120.7 %copy-start = (bf16[1024,32]{0,1:T(8,128)(2,1)S(1)}, bf16[1024,32]{0,1:T(8,128)(2,1)}, u32[]{:S(2)}) copy-start(bf16[1024,32]{0,1:T(8,128)(2,1)} %param.17) | copy-start | bytes 196612
  0.6 2.9 %copy-start.4 = (bf16[32,2048]{1,0:T(8,128)(2,1)S(1)}, bf16[32,2048]{1,0:T(8,128)(2,1)}, u32[]{:S(2)}) copy-start(bf16[32,2048]{1,0:T(8,128)(2,1)} %up_ref.1) | copy-start | bytes 393220
  0.7 2.9 %copy-start.2 = (bf16[256,2048]{1,0:T(8,128)(2,1)S(1)}, bf16[256,2048]{1,0:T(8,128)(2,1)}, u32[]{:S(2)}) copy-start(bf16[256,2048]{1,0:T(8,128)(2,1)} %cotangent_ref.1) | copy-start | bytes 3145732
  0.7 2.9 %copy-start.3 = (bf16[1024,256]{1,0:T(8,128)(2,1)S(1)}, bf16[1024,256]{1,0:T(8,128)(2,1)}, u32[]{:S(2)}) copy-start(bf16[1024,256]{1,0:T(8,128)(2,1)} %outer_ref.1) | copy-start | bytes 1572868
  3.6 118.0 %copy-start.7 = (bf16[1024,2048]{1,0:T(8,128)(2,1)S(1)}, bf16[1024,2048]{1,0:T(8,128)(2,1)}, u32[]{:S(2)}) copy-start(bf16[1024,2048]{1,0:T(8,128)(2,1)} %constant.19.clone) | copy-start | bytes 12582916
  122.9 1.6 copy-start.5
  124.5 1.6 copy-start.6
  129.0 2.2 %copy-start.1 = (bf16[1024,2048]{1,0:T(8,128)(2,1)S(1)}, bf16[1024,2048]{1,0:T(8,128)(2,1)}, u32[]{:S(2)}) copy-start(bf16[1024,2048]{1,0:T(8,128)(2,1)} %get-tuple-element.20.cotangent_any) | copy-start | bytes 12582916
  131.2 38.1 %copy-start.8 = (bf16[1024,256]{1,0:T(8,128)(2,1)S(1)}, bf16[1024,256]{1,0:T(8,128)(2,1)}, u32[]{:S(2)}) copy-start(bf16[1024,256]{1,0:T(8,128)(2,1)} %param.10) | copy-start | bytes 1572868
  131.2 38.1 %copy-start.9 = (bf16[1024,256]{1,0:T(8,128)(2,1)S(1)}, bf16[1024,256]{1,0:T(8,128)(2,1)}, u32[]{:S(2)}) copy-start(bf16[1024,256]{1,0:T(8,128)(2,1)} %param.12) | copy-start | bytes 1572868

commit v6 on v5

--- a/solution.py
+++ b/solution.py
@@ -312,7 +312,7 @@
     )(grad_gated_ch, outer_grad_ch, token_t, down_t, whole_cotangent)
 
 
-exchange_step = 4
+exchange_step = 2
 
 
 def project_kernel(

time: 172 us -> 177 us (1.029)
  Pallas kernels: 155 us -> 160 us
    pallas_call x1, Pallas kernels: 118 us -> 121 us  [project_all(): pl.pallas_call(functools.partial(project_kernel, ctx_size, tp_size), out_...]
    pallas_call x1, Pallas kernels: 37.5 us -> 39.5 us  [return_all(): pl.pallas_call(functools.partial(return_kernel, ctx_size, tp_size), out_s...]
where the time goes in v6:
time: 177 us
  Pallas kernels  160 us (90%)
  matrix products  7.97 us (5%)
  other arithmetic  4.77 us (3%)
  local copies, waits for them, and re-layouts  3.38 us (2%)
    pallas_call x1, Pallas kernels, project_all(): pl.pallas_call(functools.partial(project_kernel, ctx_size, tp_size), out_...  121 us
    pallas_call x1, Pallas kernels, return_all(): pl.pallas_call(functools.partial(return_kernel, ctx_size, tp_size), out_s...  39.5 us
    dot_general x3, matrix products, dense_spectrum(): spec = jnp.dot(field, table, preferred_element_type=jnp.float32)  3.74 us

profile of v6, /device:TPU:0, one launch (start us, length us, event | category | flops | bytes accessed | tf_op | source)
XLA Modules:
  0.0 177.1 jit_solution(17611080377445395429)
XLA Ops:
  0.6 0.0 copy-start
  0.6 0.0 copy-start.4
  0.7 0.0 copy-start.2
  0.7 0.0 copy-start.3
  0.7 1.6 select_convert_fusion.filter_ref
  2.3 1.3 fusion.5.gated_ref
  3.6 0.0 copy-done.4
  3.6 0.0 copy-done.2
  3.6 0.0 copy-done.3
  3.6 0.0 copy-start.7
  3.6 120.7 %shard_map.137 = (bf16[1024,2048]{1,0:T(8,128)(2,1)}, bf16[256,1024]{1,0:T(8,128)(2,1)S(1)}, bf16[256,1024]{1,0:T(8,128)(2,1)S(1)}, bf16[256,1024]{1,0:T(8,128)(...) custom-call(bf16[256,2048]{1,0:T(8,128)(2,1)S(1)} %copy-done.2, bf16[1024,2048]{1,0:T(8,128)(2,1)} %weight_any.1, ...), custom_call_target="tpu_custom_call" | custom-call | tf_op jit(solution)/shard_map/pallas_call | solution.py:584
  124.3 0.0 copy-done
  124.3 0.3 fusion.4
  124.6 0.0 copy-done.7
  124.7 1.2 fusion.21
  125.9 0.0 copy-start.5
  125.9 1.2 fusion.11
  127.2 0.3 copy-done.5
  127.5 0.0 copy-start.6
  127.5 0.8 fusion.13
  128.3 0.8 copy-done.6
  129.1 0.8 fusion.2.grad_ref
  129.9 1.2 fusion.22
  131.2 0.9 fusion.14
  132.0 0.0 copy-start.1
  132.0 0.9 fusion.7
  133.0 0.3 convolution_convert_fusion.1.down_ref
  133.2 0.2 convolution_convert_fusion.token_ref
  133.5 0.7 copy-done.1
  134.2 0.0 copy-start.8
  134.2 0.0 copy-start.9
  134.2 39.5 %shard_map.138 = (bf16[1024,256]{1,0:T(8,128)(2,1)S(1)}, bf16[1024,256]{1,0:T(8,128)(2,1)S(1)}, bf16[32,1024]{1,0:T(8,128)(2,1)S(1)}, f32[32,2048]{1,0:T(8,128)S(1)}) custom-call(bf16[256,1024]{1,0:T(8,128)(2,1)S(1)} %fusion.2.grad_ref, bf16[256,1024]{1,0:T(8,128)(2,1)S(1)} %get-tuple-element.27.outer_ref, ...), custom_call_target="tpu_custom_call" | custom-call | tf_op jit(solution)/shard_map/pallas_call | solution.py:285
  173.7 0.7 multiply_bitcast_fusion
  174.4 0.0 copy-done.8
  174.4 0.0 copy-done.9
  174.4 1.2 fusion.10
  175.6 0.8 copy.17
  176.4 0.7 copy.18
  (1 shorter events, 0.0 us)
Async XLA Ops:
  0.6 123.7 %copy-start = (bf16[1024,32]{0,1:T(8,128)(2,1)S(1)}, bf16[1024,32]{0,1:T(8,128)(2,1)}, u32[]{:S(2)}) copy-start(bf16[1024,32]{0,1:T(8,128)(2,1)} %param.17) | copy-start | bytes 196612
  0.6 2.9 %copy-start.4 = (bf16[32,2048]{1,0:T(8,128)(2,1)S(1)}, bf16[32,2048]{1,0:T(8,128)(2,1)}, u32[]{:S(2)}) copy-start(bf16[32,2048]{1,0:T(8,128)(2,1)} %up_ref.1) | copy-start | bytes 393220
  0.7 2.9 %copy-start.2 = (bf16[256,2048]{1,0:T(8,128)(2,1)S(1)}, bf16[256,2048]{1,0:T(8,128)(2,1)}, u32[]{:S(2)}) copy-start(bf16[256,2048]{1,0:T(8,128)(2,1)} %cotangent_ref.1) | copy-start | bytes 3145732
  0.7 2.9 %copy-start.3 = (bf16[1024,256]{1,0:T(8,128)(2,1)S(1)}, bf16[1024,256]{1,0:T(8,128)(2,1)}, u32[]{:S(2)}) copy-start(bf16[1024,256]{1,0:T(8,128)(2,1)} %outer_ref.1) | copy-start | bytes 1572868
  3.6 121.0 %copy-start.7 = (bf16[1024,2048]{1,0:T(8,128)(2,1)S(1)}, bf16[1024,2048]{1,0:T(8,128)(2,1)}, u32[]{:S(2)}) copy-start(bf16[1024,2048]{1,0:T(8,128)(2,1)} %constant.19.clone) | copy-start | bytes 12582916
  125.9 1.6 copy-start.5
  127.5 1.6 copy-start.6
  132.0 2.2 %copy-start.1 = (bf16[1024,2048]{1,0:T(8,128)(2,1)S(1)}, bf16[1024,2048]{1,0:T(8,128)(2,1)}, u32[]{:S(2)}) copy-start(bf16[1024,2048]{1,0:T(8,128)(2,1)} %get-tuple-element.20.cotangent_any) | copy-start | bytes 12582916
  134.2 40.1 %copy-start.8 = (bf16[1024,256]{1,0:T(8,128)(2,1)S(1)}, bf16[1024,256]{1,0:T(8,128)(2,1)}, u32[]{:S(2)}) copy-start(bf16[1024,256]{1,0:T(8,128)(2,1)} %param.10) | copy-start | bytes 1572868
  134.2 40.1 %copy-start.9 = (bf16[1024,256]{1,0:T(8,128)(2,1)S(1)}, bf16[1024,256]{1,0:T(8,128)(2,1)}, u32[]{:S(2)}) copy-start(bf16[1024,256]{1,0:T(8,128)(2,1)} %param.12) | copy-start | bytes 1572868
